TPU v7x, 32 devices: a whole 2x2x4 slice. The times are simulated.
32 devices in a mesh: leaf: 8 (over z, x), grp: 4 (over y, core).
Axes of the slice: x: 2, y: 2, z: 4, core: 2. Of those that a mesh axis runs over, the one named last changes fastest.
Arguments:
- vectors: float32 [16, 262144], P(None, ('leaf', 'grp')), may hold values from -6 to 6
- coords: float32 [2, 262144], P(None, ('leaf', 'grp')), may hold values from 0 to 1, as said below
- perm: int32 [262144], P(('leaf', 'grp')), may hold values from 0 to 8191, as said below
- bases: float32 [512, 64, 512], P(('leaf', 'grp')), may hold values from -0.25 to 0.25
- leaf_maps: float32 [512, 64, 64], P(('leaf', 'grp')), may hold values from -0.1875 to 0.1875
- node_maps: float32 [32, 64, 64], P(('leaf', 'grp')), may hold values from -0.375 to 0.375
- leaf_skel: float32 [512, 2, 64], P(('leaf', 'grp')), may hold values from 0 to 1
- node_skel: float32 [32, 2, 64], P(('leaf', 'grp')), may hold values from 0 to 1
- sub_skel: float32 [8, 2, 64], P('leaf'), may hold values from 0 to 1
- leaf_src: int32 [512, 16], P(('leaf', 'grp')), may hold values from 0 to 63
- leaf_count: int32 [512], P(('leaf', 'grp')), may hold values from 1 to 16
- node_src: int32 [32, 8], P(('leaf', 'grp')), may hold values from 0 to 11, as said below
- node_count: int32 [32], P(('leaf', 'grp')), may hold values from 1 to 8
Outputs:
- product: float32 [16, 262144], P(None, ('leaf', 'grp'))
Inputs may be any that keep to these rules, and one draw needn't show every extreme that they name: `perm`: each aligned block of 8192 entries holds every number of 0 to 8191 once. `coords`: rows 3k, 3k + 1 and 3k + 2 share one site's coordinates. `node_src`: entries index the device nodes of subtrees s - 1, s, s + 1 in order (s the node's own subtree), only subtrees that exist.
All inputs are finite; a program needn't handle non-finite values.
Results may differ from a plain program's by a relative error of at most 0.0003.
Values sent between devices are 32-bit elements; how exact they have to be, the bound alone decides.
No kernel may reach another device: no remote copies, remote signals or barrier semaphores. Data moves between devices by JAX's collectives and lax.ppermute only.
A program may use at most 64 MiB of HBM per device.

v0:
```python
import math

import jax
import jax.numpy as jnp
import numpy as np
from jax import lax
from jax.sharding import PartitionSpec as P


def padded(cells, sides, width):
    for axis, dim in sides:
        count = lax.axis_size(axis)
        ends = count - 1
        head = lax.slice_in_dim(cells, 0, width, axis=dim)
        tail = lax.slice_in_dim(cells, cells.shape[dim] - width, cells.shape[dim], axis=dim)
        cells = jnp.concatenate(
            [
                lax.ppermute(tail, axis, [(i, (i + 1) % count) for i in range(ends)]),
                cells,
                lax.ppermute(head, axis, [((i + 1) % count, i) for i in range(ends)]),
            ],
            axis=dim,
        )
    return cells


def make_tables():
    smooth = [0, 2, 4]
    sigmas = [1.0, 0.8, 1.2]
    rho = [[1.0, 0.5, 0.3], [0.5, 1.0, 0.4], [0.3, 0.4, 1.0]]
    scale_table = np.zeros((3, 3))
    poly_tables = np.zeros((5, 3, 3))
    for first in range(3):
        for second in range(3):
            order = (smooth[first] + smooth[second]) // 2
            scale_table[first, second] = math.sqrt(2.0 * order + 1.0) / 0.3
            amp = sigmas[first] * sigmas[second] * rho[first][second]
            for power in range(order + 1):
                kterm = order - power
                coeff = math.factorial(order) / math.factorial(2 * order)
                coeff = (
                    coeff
                    * math.factorial(order + kterm)
                    / (math.factorial(kterm) * math.factorial(order - kterm))
                )
                poly_tables[power, first, second] = amp * coeff * 2.0**power
    return (scale_table, poly_tables)


def cross_cov(coords_a, vars_a, coords_b, vars_b):
    kernel_tables = make_tables()
    diff_x = coords_a[0][:, None] - coords_b[0][None, :]
    diff_y = coords_a[1][:, None] - coords_b[1][None, :]
    dist = jnp.sqrt(diff_x * diff_x + diff_y * diff_y)
    col_zero = (vars_b == 0)[None, :]
    col_one = (vars_b == 1)[None, :]

    def lookup(table):
        rows = jnp.asarray(table, jnp.float32)[vars_a]
        return jnp.where(col_zero, rows[:, 0:1], jnp.where(col_one, rows[:, 1:2], rows[:, 2:3]))

    scaled = lookup(kernel_tables[0]) * dist
    poly = lookup(kernel_tables[1][4])
    for power in (3, 2, 1, 0):
        poly = poly * scaled + lookup(kernel_tables[1][power])
    return jnp.exp(-scaled) * poly


def couple(coef, src_skel, dst_skel, skel_var, weight):
    blocks = jax.vmap(lambda one, two: cross_cov(one, skel_var, two, skel_var))(src_skel, dst_skel)
    terms = jnp.einsum("nvr,nrq->nvq", coef, blocks, precision=lax.Precision.HIGHEST)
    return terms * weight[:, None, None] / math.sqrt(coef.shape[2])


def shards(
    vectors,
    coords,
    perm,
    bases,
    leaf_maps,
    node_maps,
    leaf_skel,
    node_skel,
    sub_skel,
    leaf_src,
    leaf_count,
    node_src,
    node_count,
):
    high = lax.Precision.HIGHEST
    nvec, rows_dev = vectors.shape
    leaves, rank, block = bases.shape
    node_len = node_src.shape[1]
    groups = lax.axis_size("grp")
    subtrees = lax.axis_size("leaf")
    device_pos = lax.axis_index("leaf") * groups + lax.axis_index("grp")
    tree_vec = jnp.take(vectors, perm, axis=1)
    tree_crd = jnp.take(coords, perm, axis=1)
    leaf_vec = tree_vec.reshape(nvec, leaves, block).transpose(1, 0, 2)
    leaf_crd = tree_crd.reshape(2, leaves, block).transpose(1, 0, 2)
    leaf_var = ((perm + device_pos * rows_dev % 3) % 3).reshape(leaves, block)
    skel_var = jnp.arange(rank, dtype=jnp.int32) % 3
    up_leaf = jnp.einsum("lvb,lrb->lvr", leaf_vec, bases, precision=high)
    group_coef, group_skel = (
        lax.all_gather(up_leaf, "grp", axis=0, tiled=True),
        lax.all_gather(leaf_skel, "grp", axis=0, tiled=True),
    )

    def owner_step(order, total):
        src = lax.dynamic_slice_in_dim(leaf_src, order, 1, 1)[:, 0]
        weight = (order < leaf_count).astype(jnp.float32)
        return total + couple(group_coef[src], group_skel[src], leaf_skel, skel_var, weight)

    far_leaf = lax.fori_loop(
        jnp.int32(0), jnp.max(leaf_count), owner_step, jnp.zeros((leaves, nvec, rank), jnp.float32)
    )
    up_node = jnp.einsum("lvr,lrq->vq", up_leaf, leaf_maps, precision=high)
    packed = jnp.concatenate([up_node[None], node_skel], axis=1)
    group_nodes = lax.all_gather(packed, "grp", axis=0, tiled=True)
    up_sub = lax.psum(jnp.dot(up_node, node_maps[0], precision=high), "grp")
    beside_all = padded(group_nodes, (("leaf", 0),), groups)
    pieces = beside_all[node_src[0]]
    node_weight = (jnp.arange(node_len, dtype=jnp.int32) < node_count[0]).astype(jnp.float32)
    node_dst = jnp.broadcast_to(node_skel[0], (node_len, 2, rank))
    far_node = couple(pieces[:, :nvec], pieces[:, nvec:], node_dst, skel_var, node_weight).sum(
        axis=0
    )
    sub_pack = jnp.concatenate([up_sub[None], sub_skel], axis=1)
    all_subs = lax.all_gather(sub_pack, "leaf", axis=0, tiled=True)
    mine = lax.axis_index("leaf")
    others = jnp.arange(subtrees, dtype=jnp.int32)
    sub_weight = (jnp.abs(others - mine) >= 2).astype(jnp.float32)
    sub_dst = jnp.broadcast_to(sub_skel[0], (subtrees, 2, rank))
    far_sub = couple(all_subs[:, :nvec], all_subs[:, nvec:], sub_dst, skel_var, sub_weight).sum(
        axis=0
    )
    down_node = far_node + jnp.dot(far_sub, node_maps[0].T, precision=high)
    down_leaf = far_leaf + jnp.einsum("vq,lrq->lvr", down_node, leaf_maps, precision=high)
    far_rows = jnp.einsum("lvr,lrb->lvb", down_leaf, bases, precision=high)

    def near_block(packed_rows):
        rows_vec, rows_crd, rows_var = packed_rows
        dense = cross_cov(rows_crd, rows_var, rows_crd, rows_var)
        return jnp.dot(rows_vec, dense, precision=high) / math.sqrt(block)

    near = lax.map(near_block, (leaf_vec, leaf_crd, leaf_var))
    tree_out = (far_rows + near).transpose(1, 0, 2).reshape(nvec, rows_dev)
    return jnp.zeros_like(vectors).at[:, perm].set(tree_out)


def solution(mesh):
    placed = (
        P(None, ("leaf", "grp")),
        P(None, ("leaf", "grp")),
        P(("leaf", "grp")),
        P(("leaf", "grp"), None, None),
        P(("leaf", "grp"), None, None),
        P(("leaf", "grp"), None, None),
        P(("leaf", "grp"), None, None),
        P(("leaf", "grp"), None, None),
        P("leaf", None, None),
        P(("leaf", "grp"), None),
        P(("leaf", "grp")),
        P(("leaf", "grp"), None),
        P(("leaf", "grp")),
    )
    return jax.shard_map(
        shards, mesh=mesh, in_specs=placed, out_specs=P(None, ("leaf", "grp")), check_vma=False
    )
```

profile of v0, /device:TPU:0, one launch (start us, length us, event | category | flops | bytes accessed | tf_op | source)
XLA Modules:
  0.0 584.4 jit_solution(2927131605807999089)
XLA Ops:
  2.4 3.5 copy.66
  5.8 29.9 %gather_fusion.8 = f32[8192,16]{1,0:T(8,128)} fusion(f32[16,8192]{0,1:T(8,128)} %copy.66, s32[8192]{0:T(1024)S(1)} %get-tuple-element.558), kind=kCustom, calls=%fused_computation.8 | custom fusion | bytes 1081344 | tf_op jit(solution)/shard_map/jit(_take)/gather | solution.py:97
  35.8 2.8 copy.67
  41.1 6.6 %all_gather.14 = f32[4,18,64]{2,1,0:T(8,128)} all-gather(f32[1,18,64]{2,1,0:T(8,128)S(1)} %pad_maximum_fusion.1), channel_id=1, replica_groups=mesh['leaf'=8,'grp'=4] {'grp'}, dimensions={0}, use_global_device_ids=true | all-gather | bytes 23040 | tf_op jit(solution)/shard_map/all_gather | solution.py:119
  47.7 4.5 collective-permute-start
  55.3 7.2 %all_gather.12 = f32[64,16,64]{2,1,0:T(8,128)S(1)} all-gather(f32[16,16,64]{2,1,0:T(8,128)S(1)} %fusion.168), channel_id=1, replica_groups=mesh['leaf'=8,'grp'=4] {'grp'}, dimensions={0}, use_global_device_ids=true | all-gather | bytes 327680 | tf_op jit(solution)/shard_map/all_gather | solution.py:105
  73.1 5.7 all_gather.13
  79.0 7.0 %psum.7 = f32[1,16,64]{2,1,0:T(8,128)S(1)} all-reduce(f32[1,16,64]{2,1,0:T(8,128)S(1)} %convolution_bitcast_fusion.1), channel_id=1, replica_groups=mesh['leaf'=8,'grp'=4] {'grp'}, use_global_device_ids=true, to_apply=%region_4.5 | all-reduce | flops 1024 | bytes 8192 | tf_op jit(solution)/shard_map/psum | solution.py:120
  86.6 32.1 %all_gather.15 = f32[8,18,64]{2,1,0:T(8,128)S(1)} all-gather(f32[1,18,64]{2,1,0:T(8,128)S(1)} %pad_maximum_fusion.2), channel_id=1, replica_groups=mesh['leaf'=8,'grp'=4] {'leaf'}, dimensions={0}, use_global_device_ids=true | all-gather | bytes 41472 | tf_op jit(solution)/shard_map/all_gather | solution.py:129
  123.2 161.8 %while.26 = (s32[]{:T(128)}, f32[16,16,64]{2,1,0:T(8,128)}, s32[]{:T(128)}, s32[16,16]{0,1:T(8,128)}, f32[64,16,64]{2,1,0:T(8,128)S(1)}, /*index=5*/f32[64,3]{0,...) while((s32[]{:T(128)}, f32[16,16,64]{2,1,0:T(8,128)}, ...), condition=%wide.region_2.3_spmd.clone.clone, body=%wide.region_1.2_spmd.clone.clone.sunk | while | flops 13731413 | bytes 625251 | solution.py:114
  285.1 3.4 copy.76
  288.4 29.9 %gather_fusion.16 = f32[8192,2]{1,0:T(8,128)} fusion(f32[2,8192]{0,1:T(8,128)} %copy.76, s32[8192]{0:T(1024)S(1)} %get-tuple-element.558), kind=kCustom, calls=%fused_computation.16 | custom fusion | bytes 163840 | tf_op jit(solution)/shard_map/jit(_take)/gather | solution.py:98
  318.3 2.8 copy.77
  321.3 223.5 %while.25 = (s32[]{:T(128)}, f32[16,16,512]{2,1,0:T(8,128)}, f32[16,16,512]{2,1,0:T(8,128)}, s32[16,512]{1,0:T(8,128)S(1)}, f32[16,2,512]{2,1,0:T(2,128)S(1)}, /...) while((s32[]{:T(128)}, f32[16,16,512]{2,1,0:T(8,128)}, ...), condition=%wide.region_7.8_spmd.clone, body=%wide.region_6.7_spmd.sunk.clone.sunk | while | flops 57683456 | bytes 556249 | solution.py:146
  331.8 3.4 fusion.190
  345.8 3.4 fusion.190
  359.8 3.4 fusion.190
  373.8 3.4 fusion.190
  387.7 3.4 fusion.190
  401.7 3.4 fusion.190
  415.7 3.4 fusion.190
  429.6 3.4 fusion.190
  443.6 3.4 fusion.190
  457.6 3.4 fusion.190
  471.5 3.4 fusion.190
  485.5 3.4 fusion.190
  499.5 3.4 fusion.190
  513.5 3.4 fusion.190
  527.4 3.4 fusion.190
  541.4 3.4 fusion.190
  557.9 23.0 %scatter_custom_fusion = f32[16,8192]{0,1:T(8,128)} fusion(s32[8192]{0:T(1024)} %get-tuple-element.559, f32[8192,16]{1,0:T(8,128)} %copy.79, f32[]{:T(128)} %constant.96.clone.1), kind=kCustom, calls=%fused_computation.168 | custom fusion | bytes 524800 | tf_op jit(solution)/shard_map/scatter | solution.py:148
  580.9 3.5 copy.80
  (639 shorter events, 353.3 us)
Async XLA Ops:
  0.0 38.8 %copy-start = (f32[16,64,512]{2,1,0:T(8,128)S(1)}, f32[16,64,512]{2,1,0:T(8,128)}, u32[]{:S(2)}) copy-start(f32[16,64,512]{2,1,0:T(8,128)} %param.44) | copy-start | bytes 6291460
  35.8 4.9 copy-start.7
  35.8 5.3 copy-start.27
  35.8 26.8 %copy-start.1 = (f32[3,3]{1,0:T(4,128)S(1)}, f32[3,3]{1,0:T(4,128)}, u32[]{:S(2)}) copy-start(f32[3,3]{1,0:T(4,128)} %constant.145.clone) | copy-start | bytes 112
  35.8 28.7 %copy-start.2 = (f32[3,3]{1,0:T(4,128)S(1)}, f32[3,3]{1,0:T(4,128)}, u32[]{:S(2)}) copy-start(f32[3,3]{1,0:T(4,128)} %constant.146.clone) | copy-start | bytes 112
  35.8 29.3 %copy-start.3 = (f32[3,3]{1,0:T(4,128)S(1)}, f32[3,3]{1,0:T(4,128)}, u32[]{:S(2)}) copy-start(f32[3,3]{1,0:T(4,128)} %constant.147.clone) | copy-start | bytes 112
  38.6 29.2 %copy-start.4 = (f32[3,3]{1,0:T(4,128)S(1)}, f32[3,3]{1,0:T(4,128)}, u32[]{:S(2)}) copy-start(f32[3,3]{1,0:T(4,128)} %constant.148.clone) | copy-start | bytes 112
  38.6 29.8 %copy-start.5 = (f32[3,3]{1,0:T(4,128)S(1)}, f32[3,3]{1,0:T(4,128)}, u32[]{:S(2)}) copy-start(f32[3,3]{1,0:T(4,128)} %constant.149.clone) | copy-start | bytes 112
  38.6 32.5 %copy-start.6 = (f32[3,3]{1,0:T(4,128)S(1)}, f32[3,3]{1,0:T(4,128)}, u32[]{:S(2)}) copy-start(f32[3,3]{1,0:T(4,128)} %constant.150.clone) | copy-start | bytes 112
  38.7 34.5 %copy-start.21 = (f32[16,2,64]{2,1,0:T(2,128)S(1)}, f32[16,2,64]{2,1,0:T(2,128)}, u32[]{:S(2)}) copy-start(f32[16,2,64]{2,1,0:T(2,128)} %param.47) | copy-start | bytes 24580
  38.7 40.2 %copy-start.12 = (f32[1,64,64]{2,1,0:T(8,128)S(1)}, f32[1,64,64]{2,1,0:T(8,128)}, u32[]{:S(2)}) copy-start(f32[1,64,64]{2,1,0:T(8,128)} %param.46) | copy-start | bytes 49156
  38.7 47.3 %copy-start.28 = (f32[1,2,64]{2,1,0:T(2,128)S(1)}, f32[1,2,64]{2,1,0:T(2,128)}, u32[]{:S(2)}) copy-start(f32[1,2,64]{2,1,0:T(2,128)} %param.49) | copy-start | bytes 1540
  38.7 80.6 %copy-start.29 = (s32[1,8]{1,0:T(1,128)S(1)}, s32[1,8]{1,0:T(1,128)}, u32[]{:S(2)}) copy-start(s32[1,8]{1,0:T(1,128)} %param.52) | copy-start | bytes 100
  38.7 81.9 %copy-start.26 = (s32[16,16]{1,0:T(8,128)S(1)}, s32[16,16]{1,0:T(8,128)}, u32[]{:S(2)}) copy-start(s32[16,16]{1,0:T(8,128)} %param.50) | copy-start | bytes 3076
  38.8 16.0 %copy-start.19 = (pred[16,512]{1,0:T(8,128)(4,1)}, pred[16,512]{1,0:T(8,128)(4,1)S(1)}, u32[]{:S(2)}) copy-start(pred[16,512]{1,0:T(8,128)(4,1)S(1)} %broadcast_in_dim.878) | copy-start | bytes 24580
  38.9 15.9 %copy-start.8 = (f32[16,16,512]{2,1,0:T(8,128)}, f32[16,16,512]{2,1,0:T(8,128)S(1)}, u32[]{:S(2)}) copy-start(f32[16,16,512]{2,1,0:T(8,128)S(1)} %select_bitcast_fusion) | copy-start | bytes 1572868
  47.7 500.3 %collective-permute-start = (f32[4,18,64]{2,1,0:T(8,128)}, f32[4,18,64]{2,1,0:T(8,128)}, u32[]{:S(2)}, u32[]{:S(2)}) collective-permute-start(f32[4,18,64]{2,1,0:T(8,128)} %all_gather.14), channel_id=1, source_target_pairs={{0,4},{4,8},{8,12},{12,16},{16,20},{20,24},{24,28},{1,5},{5,9},{9,... | collective-permute-start | bytes 55304 | tf_op jit(solution)/shard_map/ppermute | solution.py:18
  52.2 495.8 %collective-permute-start.1 = (f32[4,18,64]{2,1,0:T(8,128)}, f32[4,18,64]{2,1,0:T(8,128)}, u32[]{:S(2)}, u32[]{:S(2)}) collective-permute-start(f32[4,18,64]{2,1,0:T(8,128)} %all_gather.14), channel_id=1, source_target_pairs={{4,0},{8,4},{12,8},{16,12},{20,16},{24,20},{28,24},{5,1},{9,5},{13... | collective-permute-start | bytes 55304 | tf_op jit(solution)/shard_map/ppermute | solution.py:20
  118.7 4.6 copy-start.15
  285.0 36.1 %copy-start.20 = (pred[16,512]{1,0:T(8,128)(4,1)S(1)}, pred[16,512]{1,0:T(8,128)(4,1)}, u32[]{:S(2)}) copy-start(pred[16,512]{1,0:T(8,128)(4,1)} %copy-done.19) | copy-start | bytes 24580
  285.1 36.2 %copy-start.14 = (s32[8192]{0:T(1024)S(1)}, s32[8192]{0:T(1024)}, u32[]{:S(2)}) copy-start(s32[8192]{0:T(1024)} %get-tuple-element.557) | copy-start | bytes 98308
  321.3 225.4 %copy-start.16 = (f32[8,18,64]{2,1,0:T(8,128)S(1)}, f32[8,18,64]{2,1,0:T(8,128)}, u32[]{:S(2)}) copy-start(f32[8,18,64]{2,1,0:T(8,128)} %copy-done.15) | copy-start | bytes 110596
  321.3 231.3 %copy-start.13 = (f32[1,64,64]{2,1,0:T(8,128)S(1)}, f32[1,64,64]{2,1,0:T(8,128)}, u32[]{:S(2)}) copy-start(f32[1,64,64]{2,1,0:T(8,128)} %param.46) | copy-start | bytes 49156
  321.3 231.5 %copy-start.10 = (f32[16,16,64]{2,1,0:T(8,128)S(1)}, f32[16,16,64]{2,1,0:T(8,128)}, u32[]{:S(2)}) copy-start(f32[16,16,64]{2,1,0:T(8,128)} %get-tuple-element.280) | copy-start | bytes 196612
  331.8 3.4 copy-start.18
  345.8 3.4 copy-start.18
  359.8 3.4 copy-start.18
  387.7 3.4 copy-start.18
  429.6 3.4 copy-start.18
  471.5 3.4 copy-start.18
  513.4 3.4 copy-start.18
  544.8 9.3 %copy-start.9 = (f32[16,16,512]{2,1,0:T(8,128)S(1)}, f32[16,16,512]{2,1,0:T(8,128)}, u32[]{:S(2)}) copy-start(f32[16,16,512]{2,1,0:T(8,128)} %get-tuple-element.281) | copy-start | bytes 1572868
  (45 other events, 79.0 us)
where the time goes:
time: 591 us; the launch traced here: 584 us
  local copies, waits for them, and re-layouts  354 us (60%)
  matrix products  104 us (18%)
  blocking collectives  58.6 us (10%)
  other arithmetic  47.3 us (8%)
  loops' own time  13.2 us (2%)
    gather x102, local copies, waits for them, and re-layouts, lookup(): rows = jnp.asarray(table, jnp.float32)[vars_a]  103 us
    dot_general x16, matrix products, near_block(): return jnp.dot(rows_vec, dense, precision=high) / math.sqrt(block)  54.8 us
    slice x52, local copies, waits for them, and re-layouts, lookup(): rows[:, 0:1]  49.7 us
    dot_general x18, matrix products, couple(): jnp.einsum('nvr,nrq->nvq', coef, blocks, precision=lax.Precision.HIGHEST)  44.5 us
    broadcast_in_dim x48, local copies, waits for them, and re-layouts, lookup(): jnp.where(col_zero, rows[:, 0:1], jnp.where(col_one, rows[:, 1:2], rows[:...  38.2 us
    gather x2, local copies, waits for them, and re-layouts, shards(): tree_vec = jnp.take(vectors, perm, axis=1)  32.8 us
    gather x2, local copies, waits for them, and re-layouts, shards(): tree_crd = jnp.take(coords, perm, axis=1)  32.7 us
    all_gather x1, blocking collectives, shards(): all_subs = lax.all_gather(sub_pack, 'leaf', axis=0, tiled=True)  32.1 us
  transfers between devices with their start and end apart: 2, of which 0 were waited for; matrix products, arithmetic and copies ran while one was open for 72% of the time, Pallas kernels for 0%

commit v1 on v0

--- a/solution.py
+++ b/solution.py
@@ -5,23 +5,6 @@
 import numpy as np
 from jax import lax
 from jax.sharding import PartitionSpec as P
-
-
-def padded(cells, sides, width):
-    for axis, dim in sides:
-        count = lax.axis_size(axis)
-        ends = count - 1
-        head = lax.slice_in_dim(cells, 0, width, axis=dim)
-        tail = lax.slice_in_dim(cells, cells.shape[dim] - width, cells.shape[dim], axis=dim)
-        cells = jnp.concatenate(
-            [
-                lax.ppermute(tail, axis, [(i, (i + 1) % count) for i in range(ends)]),
-                cells,
-                lax.ppermute(head, axis, [((i + 1) % count, i) for i in range(ends)]),
-            ],
-            axis=dim,
-        )
-    return cells
 
 
 def make_tables():
@@ -101,10 +84,25 @@
     leaf_var = ((perm + device_pos * rows_dev % 3) % 3).reshape(leaves, block)
     skel_var = jnp.arange(rank, dtype=jnp.int32) % 3
     up_leaf = jnp.einsum("lvb,lrb->lvr", leaf_vec, bases, precision=high)
-    group_coef, group_skel = (
-        lax.all_gather(up_leaf, "grp", axis=0, tiled=True),
-        lax.all_gather(leaf_skel, "grp", axis=0, tiled=True),
+    grp_pos = lax.axis_index("grp")
+    mine = lax.axis_index("leaf")
+    leaf_pack = jnp.concatenate([up_leaf, leaf_skel], axis=1)
+    leaf_slots = jnp.zeros((groups * leaves, nvec + 2, rank), jnp.float32)
+    leaf_slots = lax.dynamic_update_slice(leaf_slots, leaf_pack, (grp_pos * leaves, 0, 0))
+    group_all = lax.psum(leaf_slots, "grp")
+    group_coef, group_skel = group_all[:, :nvec], group_all[:, nvec:]
+    up_node = jnp.einsum("lvr,lrq->vq", up_leaf, leaf_maps, precision=high)
+    node_pack = jnp.concatenate([up_node[None], node_skel], axis=1)
+    sub_part = jnp.dot(up_node, node_maps[0], precision=high)
+    sub_pack = jnp.concatenate(
+        [sub_part[None], jnp.where(grp_pos == 0, sub_skel, 0.0)], axis=1
     )
+    nodes = subtrees * groups
+    slots = jnp.zeros((nodes + subtrees, nvec + 2, rank), jnp.float32)
+    slots = lax.dynamic_update_slice(slots, node_pack, (device_pos, 0, 0))
+    slots = lax.dynamic_update_slice(slots, sub_pack, (nodes + mine, 0, 0))
+    tree_all = lax.psum(slots, ("leaf", "grp"))
+    all_subs = tree_all[nodes:]
 
     def owner_step(order, total):
         src = lax.dynamic_slice_in_dim(leaf_src, order, 1, 1)[:, 0]
@@ -114,20 +112,13 @@
     far_leaf = lax.fori_loop(
         jnp.int32(0), jnp.max(leaf_count), owner_step, jnp.zeros((leaves, nvec, rank), jnp.float32)
     )
-    up_node = jnp.einsum("lvr,lrq->vq", up_leaf, leaf_maps, precision=high)
-    packed = jnp.concatenate([up_node[None], node_skel], axis=1)
-    group_nodes = lax.all_gather(packed, "grp", axis=0, tiled=True)
-    up_sub = lax.psum(jnp.dot(up_node, node_maps[0], precision=high), "grp")
-    beside_all = padded(group_nodes, (("leaf", 0),), groups)
-    pieces = beside_all[node_src[0]]
+    beside = jnp.clip(node_src[0] + (mine - 1) * groups, 0, nodes - 1)
+    pieces = tree_all[beside]
     node_weight = (jnp.arange(node_len, dtype=jnp.int32) < node_count[0]).astype(jnp.float32)
     node_dst = jnp.broadcast_to(node_skel[0], (node_len, 2, rank))
     far_node = couple(pieces[:, :nvec], pieces[:, nvec:], node_dst, skel_var, node_weight).sum(
         axis=0
     )
-    sub_pack = jnp.concatenate([up_sub[None], sub_skel], axis=1)
-    all_subs = lax.all_gather(sub_pack, "leaf", axis=0, tiled=True)
-    mine = lax.axis_index("leaf")
     others = jnp.arange(subtrees, dtype=jnp.int32)
     sub_weight = (jnp.abs(others - mine) >= 2).astype(jnp.float32)
     sub_dst = jnp.broadcast_to(sub_skel[0], (subtrees, 2, rank))

time: 591 us -> 498 us (0.84)
  blocking collectives: 58.6 us -> 0 us
  local copies, waits for them, and re-layouts: 354 us -> 327 us
  other arithmetic: 47.3 us -> 32.1 us
  between operations: 1.13 us -> 14.4 us
    all_gather x4 -> x0, blocking collectives: 51.6 us -> none  [the longest x1 32.1 us: shards(): all_subs = lax.all_gather(sub_pack, 'leaf', axis=0, tiled=True)]
    gather x16, local copies, waits for them, and re-layouts: 22.8 us -> 9.41 us  [owner_step(): group_skel[src]]
    eq x32, other arithmetic: 12.1 us -> 0.7 us  [cross_cov(): col_zero = (vars_b == 0)[None, :]]
    slice x52, local copies, waits for them, and re-layouts: 49.7 us -> 38.4 us  [lookup(): rows[:, 0:1]]
    while x96 -> x32, local copies, waits for them, and re-layouts: 9.3 us -> 0.06 us
    psum x1 -> x0, blocking collectives: 7.01 us -> none  [shards(): up_sub = lax.psum(jnp.dot(up_node, node_maps[0], precision=high), 'grp')]
    unnamed x64 -> x48, local copies, waits for them, and re-layouts: 11.6 us -> 14 us
  transfers between devices with their start and end apart: 2 -> 2, of which waited for: 0 -> 0; matrix products, arithmetic and copies ran while one was open for 72% -> 50% of each run, Pallas kernels for 0% -> 0%
where the time goes in v1:
time: 498 us; the launch traced here: 493 us
  local copies, waits for them, and re-layouts  327 us (66%)
  matrix products  106 us (21%)
  other arithmetic  32.1 us (6%)
  between operations  14.4 us (3%)
  loops' own time  13.8 us (3%)
    gather x102, local copies, waits for them, and re-layouts, lookup(): rows = jnp.asarray(table, jnp.float32)[vars_a]  103 us
    dot_general x16, matrix products, near_block(): return jnp.dot(rows_vec, dense, precision=high) / math.sqrt(block)  54.7 us
    dot_general x18, matrix products, couple(): jnp.einsum('nvr,nrq->nvq', coef, blocks, precision=lax.Precision.HIGHEST)  43.7 us
    broadcast_in_dim x48, local copies, waits for them, and re-layouts, lookup(): jnp.where(col_zero, rows[:, 0:1], jnp.where(col_one, rows[:, 1:2], rows[:...  39.1 us
    slice x52, local copies, waits for them, and re-layouts, lookup(): rows[:, 0:1]  38.4 us
    gather x2, local copies, waits for them, and re-layouts, shards(): tree_crd = jnp.take(coords, perm, axis=1)  32.8 us
    gather x2, local copies, waits for them, and re-layouts, shards(): tree_vec = jnp.take(vectors, perm, axis=1)  32.8 us
    scatter x2, local copies, waits for them, and re-layouts, shards(): return jnp.zeros_like(vectors).at[:, perm].set(tree_out)  26.5 us
  transfers between devices with their start and end apart: 2, of which 0 were waited for; matrix products, arithmetic and copies ran while one was open for 50% of the time, Pallas kernels for 0%

profile of v1, /device:TPU:0, one launch (start us, length us, event | category | flops | bytes accessed | tf_op | source)
XLA Modules:
  0.0 493.2 jit_solution(4726741631674463436)
XLA Ops:
  8.9 3.5 copy.66
  12.3 29.9 %gather_fusion.8 = f32[8192,16]{1,0:T(8,128)} fusion(f32[16,8192]{0,1:T(8,128)} %copy.66, s32[8192]{0:T(1024)S(1)} %get-tuple-element.558), kind=kCustom, calls=%fused_computation.8 | custom fusion | bytes 1081344 | tf_op jit(solution)/shard_map/jit(_take)/gather | solution.py:80
  42.3 2.8 copy.67
  63.6 3.4 copy.76
  67.0 29.9 %gather_fusion.16 = f32[8192,2]{1,0:T(8,128)} fusion(f32[2,8192]{0,1:T(8,128)} %copy.76, s32[8192]{0:T(1024)S(1)} %get-tuple-element.558), kind=kCustom, calls=%fused_computation.16 | custom fusion | bytes 163840 | tf_op jit(solution)/shard_map/jit(_take)/gather | solution.py:81
  96.9 2.8 copy.77
  99.9 193.9 %while.25 = (s32[]{:T(128)}, f32[16,16,512]{2,1,0:T(8,128)}, f32[16,16,512]{2,1,0:T(8,128)}, s32[16,512]{1,0:T(8,128)S(1)}, f32[16,2,512]{2,1,0:T(2,128)S(1)}, /...) while((s32[]{:T(128)}, f32[16,16,512]{2,1,0:T(8,128)}, ...), condition=%wide.region_8.9_spmd.clone, body=%wide.region_7.8_spmd.sunk.clone.sunk | while | flops 57683456 | bytes 294049 | solution.py:137
  108.6 3.4 fusion.190
  120.7 3.4 fusion.190
  132.8 3.4 fusion.190
  144.9 3.4 fusion.190
  157.0 3.4 fusion.190
  169.2 3.4 fusion.190
  181.3 3.4 fusion.190
  193.4 3.4 fusion.190
  205.5 3.4 fusion.190
  217.6 3.4 fusion.190
  229.7 3.4 fusion.190
  241.9 3.4 fusion.190
  254.0 3.4 fusion.190
  266.1 3.4 fusion.190
  278.2 3.4 fusion.190
  290.3 3.4 fusion.190
  302.8 150.0 %while.26 = (s32[]{:T(128)}, f32[16,16,64]{2,1,0:T(8,128)}, s32[]{:T(128)}, s32[16,16]{0,1:T(8,128)}, f32[64,16,64]{2,1,0:T(8,128)S(1)}, /*index=5*/f32[64,3]{0,...) while((s32[]{:T(128)}, f32[16,16,64]{2,1,0:T(8,128)}, ...), condition=%wide.region_3.4_spmd.clone.clone, body=%wide.region_2.3_spmd.clone.clone.sunk | while | flops 13731413 | bytes 625251 | solution.py:112
  309.6 2.6 fusion.195
  318.9 2.6 fusion.195
  365.5 2.6 fusion.195
  374.8 2.6 fusion.195
  412.0 2.6 fusion.195
  421.4 2.6 fusion.195
  459.9 23.0 %scatter_custom_fusion = f32[16,8192]{0,1:T(8,128)} fusion(s32[8192]{0:T(1024)} %get-tuple-element.559, f32[8192,16]{1,0:T(8,128)} %copy.79, f32[]{:T(128)} %constant.95.clone.1), kind=kCustom, calls=%fused_computation.168 | custom fusion | bytes 524800 | tf_op jit(solution)/shard_map/scatter | solution.py:139
  482.9 3.5 copy.80
  (561 shorter events, 295.8 us)
Async XLA Ops:
  6.5 39.5 %copy-start = (f32[16,64,512]{2,1,0:T(8,128)S(1)}, f32[16,64,512]{2,1,0:T(8,128)}, u32[]{:S(2)}) copy-start(f32[16,64,512]{2,1,0:T(8,128)} %param.44) | copy-start | bytes 6291460
  6.5 288.2 %all-reduce.5.cloned.1.call-start = ((), (), s32[]{:S(2)}) async-start(), calls=%async_computation.1 | async-start | bytes 983040 | tf_op jit(solution)/shard_map/psum | solution.py:104
  42.3 5.7 %copy-start.8 = (f32[16,64,64]{2,1,0:T(8,128)S(1)}, f32[16,64,64]{2,1,0:T(8,128)}, u32[]{:S(2)}) copy-start(f32[16,64,64]{2,1,0:T(8,128)} %param.45) | copy-start | bytes 786436
  42.3 6.1 %copy-start.14 = (f32[1,64,64]{2,1,0:T(8,128)S(1)}, f32[1,64,64]{2,1,0:T(8,128)}, u32[]{:S(2)}) copy-start(f32[1,64,64]{2,1,0:T(8,128)} %param.46) | copy-start | bytes 49156
  42.3 6.2 %copy-start.18 = (f32[1,2,64]{2,1,0:T(2,128)S(1)}, f32[1,2,64]{2,1,0:T(2,128)}, u32[]{:S(2)}) copy-start(f32[1,2,64]{2,1,0:T(2,128)} %param.49) | copy-start | bytes 1540
  42.3 6.4 %copy-start.17 = (f32[1,2,64]{2,1,0:T(2,128)S(1)}, f32[1,2,64]{2,1,0:T(2,128)}, u32[]{:S(2)}) copy-start(f32[1,2,64]{2,1,0:T(2,128)} %param.48) | copy-start | bytes 1540
  45.1 8.1 %copy-start.1 = (f32[3,3]{1,0:T(4,128)S(1)}, f32[3,3]{1,0:T(4,128)}, u32[]{:S(2)}) copy-start(f32[3,3]{1,0:T(4,128)} %constant.161.clone) | copy-start | bytes 112
  45.1 9.5 %copy-start.2 = (f32[3,3]{1,0:T(4,128)S(1)}, f32[3,3]{1,0:T(4,128)}, u32[]{:S(2)}) copy-start(f32[3,3]{1,0:T(4,128)} %constant.162.clone) | copy-start | bytes 112
  45.1 10.1 %copy-start.3 = (f32[3,3]{1,0:T(4,128)S(1)}, f32[3,3]{1,0:T(4,128)}, u32[]{:S(2)}) copy-start(f32[3,3]{1,0:T(4,128)} %constant.163.clone) | copy-start | bytes 112
  45.2 12.2 %copy-start.4 = (f32[3,3]{1,0:T(4,128)S(1)}, f32[3,3]{1,0:T(4,128)}, u32[]{:S(2)}) copy-start(f32[3,3]{1,0:T(4,128)} %constant.164.clone) | copy-start | bytes 112
  46.1 11.9 %copy-start.5 = (f32[3,3]{1,0:T(4,128)S(1)}, f32[3,3]{1,0:T(4,128)}, u32[]{:S(2)}) copy-start(f32[3,3]{1,0:T(4,128)} %constant.165.clone) | copy-start | bytes 112
  46.1 14.1 %copy-start.6 = (f32[3,3]{1,0:T(4,128)S(1)}, f32[3,3]{1,0:T(4,128)}, u32[]{:S(2)}) copy-start(f32[3,3]{1,0:T(4,128)} %constant.166.clone) | copy-start | bytes 112
  46.1 15.5 %copy-start.15 = (f32[16,2,64]{2,1,0:T(2,128)S(1)}, f32[16,2,64]{2,1,0:T(2,128)}, u32[]{:S(2)}) copy-start(f32[16,2,64]{2,1,0:T(2,128)} %param.47) | copy-start | bytes 24580
  46.1 16.9 %copy-start.16 = (s32[16,16]{1,0:T(8,128)S(1)}, s32[16,16]{1,0:T(8,128)}, u32[]{:S(2)}) copy-start(s32[16,16]{1,0:T(8,128)} %param.50) | copy-start | bytes 3076
  49.5 250.6 %all-reduce.3.cloned.1.call-start = ((), (), s32[]{:S(2)}) async-start(), calls=%async_computation | async-start | bytes 1572864 | tf_op jit(solution)/shard_map/psum | solution.py:92
  99.8 193.9 %copy-start.19 = (s32[16]{0:T(128)S(1)}, s32[16]{0:T(128)}, u32[]{:S(2)}) copy-start(s32[16]{0:T(128)} %param.51) | copy-start | bytes 196
  302.8 150.0 %copy-start.9 = (f32[16,64,64]{2,1,0:T(8,128)S(1)}, f32[16,64,64]{2,1,0:T(8,128)}, u32[]{:S(2)}) copy-start(f32[16,64,64]{2,1,0:T(8,128)} %param.45) | copy-start | bytes 786436
  307.0 1.2 copy-start.13
  316.3 1.2 copy-start.13
  325.6 1.2 copy-start.13
  334.9 1.2 copy-start.13
  344.3 1.2 copy-start.13
  353.6 1.2 copy-start.13
  362.9 1.2 copy-start.13
  372.2 1.2 copy-start.13
  381.5 1.2 copy-start.13
  390.8 1.2 copy-start.13
  400.1 1.2 copy-start.13
  409.5 1.2 copy-start.13
  428.1 1.2 copy-start.13
  437.4 1.2 copy-start.13
  446.7 1.2 copy-start.13
  (5 other events, 4.4 us)
Sparse Core Ops, SparseCore 0:
  49.6 129.4 all-reduce.4
  181.6 34.6 all-reduce.2

commit v2 on v1

--- a/solution.py
+++ b/solution.py
@@ -87,22 +87,19 @@
     grp_pos = lax.axis_index("grp")
     mine = lax.axis_index("leaf")
     leaf_pack = jnp.concatenate([up_leaf, leaf_skel], axis=1)
-    leaf_slots = jnp.zeros((groups * leaves, nvec + 2, rank), jnp.float32)
-    leaf_slots = lax.dynamic_update_slice(leaf_slots, leaf_pack, (grp_pos * leaves, 0, 0))
-    group_all = lax.psum(leaf_slots, "grp")
+    group_all = lax.all_gather(leaf_pack, "grp", axis=0, tiled=True)
     group_coef, group_skel = group_all[:, :nvec], group_all[:, nvec:]
     up_node = jnp.einsum("lvr,lrq->vq", up_leaf, leaf_maps, precision=high)
     node_pack = jnp.concatenate([up_node[None], node_skel], axis=1)
     sub_part = jnp.dot(up_node, node_maps[0], precision=high)
-    sub_pack = jnp.concatenate(
-        [sub_part[None], jnp.where(grp_pos == 0, sub_skel, 0.0)], axis=1
+    sub_pack = jnp.concatenate([sub_part[None], sub_skel], axis=1)
+    nodes = subtrees * groups
+    pack = jnp.concatenate([node_pack, sub_pack], axis=2)
+    tree_all = lax.all_to_all(
+        jnp.broadcast_to(pack, (nodes,) + pack.shape[1:]), ("leaf", "grp"), 0, 0, tiled=True
     )
-    nodes = subtrees * groups
-    slots = jnp.zeros((nodes + subtrees, nvec + 2, rank), jnp.float32)
-    slots = lax.dynamic_update_slice(slots, node_pack, (device_pos, 0, 0))
-    slots = lax.dynamic_update_slice(slots, sub_pack, (nodes + mine, 0, 0))
-    tree_all = lax.psum(slots, ("leaf", "grp"))
-    all_subs = tree_all[nodes:]
+    subs = tree_all[:, :, rank:].reshape(subtrees, groups, nvec + 2, rank)
+    all_subs = jnp.concatenate([subs[:, :, :nvec].sum(axis=1), subs[:, 0, nvec:]], axis=1)
 
     def owner_step(order, total):
         src = lax.dynamic_slice_in_dim(leaf_src, order, 1, 1)[:, 0]
@@ -113,7 +110,7 @@
         jnp.int32(0), jnp.max(leaf_count), owner_step, jnp.zeros((leaves, nvec, rank), jnp.float32)
     )
     beside = jnp.clip(node_src[0] + (mine - 1) * groups, 0, nodes - 1)
-    pieces = tree_all[beside]
+    pieces = tree_all[:, :, :rank][beside]
     node_weight = (jnp.arange(node_len, dtype=jnp.int32) < node_count[0]).astype(jnp.float32)
     node_dst = jnp.broadcast_to(node_skel[0], (node_len, 2, rank))
     far_node = couple(pieces[:, :nvec], pieces[:, nvec:], node_dst, skel_var, node_weight).sum(

time: 498 us -> 411 us (0.83)
  local copies, waits for them, and re-layouts: 327 us -> 284 us
  matrix products: 106 us -> 81.2 us
  other arithmetic: 32.1 us -> 10.2 us
  between operations: 14.4 us -> 1.21 us
  blocking collectives: 0 us -> 9.8 us
  starting transfers between devices: 0.22 us -> 7.3 us
    broadcast_in_dim x48, local copies, waits for them, and re-layouts: 39.1 us -> 0.3 us  [lookup(): jnp.where(col_zero, rows[:, 0:1], jnp.where(col_one, rows[:, 1:2], rows[:...]
    dot_general x18, matrix products: 43.7 us -> 19.5 us  [couple(): jnp.einsum('nvr,nrq->nvq', coef, blocks, precision=lax.Precision.HIGHEST)]
    gather x16, local copies, waits for them, and re-layouts: 11 us -> 25.6 us  [owner_step(): group_coef[src]]
    slice x36 -> x35, local copies, waits for them, and re-layouts: 12.5 us -> 1.63 us  [cross_cov(): diff_x = coords_a[0][:, None] - coords_b[0][None, :]]
    select_n x16, other arithmetic: 10.9 us -> 0.19 us  [owner_step(): group_coef[src]]
    convert_element_type x16, other arithmetic: 10.6 us -> 0.07 us  [owner_step(): weight = (order < leaf_count).astype(jnp.float32)]
    all_gather x0 -> x1, blocking collectives: none -> 9.8 us  [shards(): group_all = lax.all_gather(leaf_pack, 'grp', axis=0, tiled=True)]
    all_to_all x0 -> x1, starting transfers between devices: none -> 7.3 us  [shards(): lax.all_to_all(jnp.broadcast_to(pack, (nodes,) + pack.shape[1:]), ('leaf'...]
  transfers between devices with their start and end apart: 2 -> 1, of which waited for: 0 -> 0; matrix products, arithmetic and copies ran while one was open for 50% -> 73% of each run, Pallas kernels for 0% -> 0%
where the time goes in v2:
time: 411 us; the launch traced here: 408 us
  local copies, waits for them, and re-layouts  284 us (69%)
  matrix products  81.2 us (20%)
  loops' own time  14.7 us (4%)
  other arithmetic  10.2 us (2%)
  blocking collectives  9.8 us (2%)
  starting transfers between devices  7.3 us (2%)
    gather x102, local copies, waits for them, and re-layouts, lookup(): rows = jnp.asarray(table, jnp.float32)[vars_a]  103 us
    dot_general x16, matrix products, near_block(): return jnp.dot(rows_vec, dense, precision=high) / math.sqrt(block)  54.7 us
    slice x52, local copies, waits for them, and re-layouts, lookup(): rows[:, 0:1]  39.6 us
    gather x2, local copies, waits for them, and re-layouts, shards(): tree_vec = jnp.take(vectors, perm, axis=1)  32.8 us
    gather x2, local copies, waits for them, and re-layouts, shards(): tree_crd = jnp.take(coords, perm, axis=1)  32.7 us
    scatter x2, local copies, waits for them, and re-layouts, shards(): return jnp.zeros_like(vectors).at[:, perm].set(tree_out)  26.5 us
    gather x16, local copies, waits for them, and re-layouts, owner_step(): group_coef[src]  25.6 us
    dot_general x18, matrix products, couple(): jnp.einsum('nvr,nrq->nvq', coef, blocks, precision=lax.Precision.HIGHEST)  19.5 us
  transfers between devices with their start and end apart: 1, of which 0 were waited for; matrix products, arithmetic and copies ran while one was open for 73% of the time, Pallas kernels for 0%

profile of v2, /device:TPU:0, one launch (start us, length us, event | category | flops | bytes accessed | tf_op | source)
XLA Modules:
  0.0 408.2 jit_solution(13260099214010276776)
XLA Ops:
  1.7 3.5 copy.121
  5.2 29.9 %gather_fusion.8 = f32[8192,16]{1,0:T(8,128)} fusion(f32[16,8192]{0,1:T(8,128)} %copy.121, s32[8192]{0:T(1024)S(1)} %get-tuple-element.600), kind=kCustom, calls=%fused_computation.8 | custom fusion | bytes 1081344 | tf_op jit(solution)/shard_map/jit(_take)/gather | solution.py:80
  35.2 2.8 copy.122
  38.2 1.8 fusion.168
  41.5 7.3 %all-to-all-start = ((f32[32,18,128]{2,1,0:T(8,128)}), f32[32,18,128]{2,1,0:T(8,128)S(1)}, u32[]{:S(2)}, u32[]{:S(2)}) async-start(f32[32,18,128]{2,1,0:T(8,128)} %broadcast_in_dim.891), calls=%async_computation | async-start | bytes 786432 | tf_op jit(solution)/shard_map/all_to_all | solution.py:98
  50.7 9.8 %all_gather.3 = f32[64,18,64]{2,0,1:T(8,128)S(1)} all-gather(f32[16,18,64]{2,0,1:T(8,128)S(1)} %copy.123), channel_id=1, replica_groups=mesh['leaf'=8,'grp'=4] {'grp'}, dimensions={0}, use_global_device_ids=true | all-gather | bytes 368640 | tf_op jit(solution)/shard_map/all_gather | solution.py:90
  69.1 70.8 %while.26 = (s32[]{:T(128)}, f32[16,16,64]{2,1,0:T(8,128)S(1)}, s32[]{:T(128)}, s32[16,16]{0,1:T(8,128)S(1)}, f32[64,16,64]{2,1,0:T(8,128)}, /*index=5*/f32[64,3...) while((s32[]{:T(128)}, f32[16,16,64]{2,1,0:T(8,128)S(1)}, ...), condition=%wide.region_2.3_spmd.clone.clone, body=%wide.region_1.2_spmd.clone.clone.sunk | while | flops 13731413 | bytes 608839 | solution.py:109
  139.9 2.6 copy.136
  142.5 29.9 %gather_fusion.16 = f32[8192,2]{1,0:T(8,128)} fusion(f32[2,8192]{0,1:T(8,128)} %copy.136, s32[8192]{0:T(1024)S(1)} %get-tuple-element.600), kind=kCustom, calls=%fused_computation.16 | custom fusion | bytes 163840 | tf_op jit(solution)/shard_map/jit(_take)/gather | solution.py:81
  172.4 2.8 copy.137
  175.4 193.8 %while.25 = (s32[]{:T(128)}, f32[16,16,512]{2,1,0:T(8,128)}, f32[16,16,512]{2,1,0:T(8,128)}, s32[16,512]{1,0:T(8,128)S(1)}, f32[16,2,512]{2,1,0:T(2,128)S(1)}, /...) while((s32[]{:T(128)}, f32[16,16,512]{2,1,0:T(8,128)}, ...), condition=%wide.region_7.8_spmd.clone, body=%wide.region_6.7_spmd.sunk.clone.sunk | while | flops 57683456 | bytes 294049 | solution.py:134
  184.1 3.4 fusion.190
  196.3 3.4 fusion.190
  208.4 3.4 fusion.190
  220.5 3.4 fusion.190
  232.6 3.4 fusion.190
  244.7 3.4 fusion.190
  256.8 3.4 fusion.190
  268.9 3.4 fusion.190
  281.0 3.4 fusion.190
  293.1 3.4 fusion.190
  305.3 3.4 fusion.190
  317.4 3.4 fusion.190
  329.5 3.4 fusion.190
  341.6 3.4 fusion.190
  353.7 3.4 fusion.190
  365.8 3.4 fusion.190
  374.7 2.2 fusion.96
  376.9 2.2 fusion.95
  379.1 2.6 copy.139
  381.7 23.0 %scatter_custom_fusion = f32[16,8192]{0,1:T(8,128)} fusion(s32[8192]{0:T(1024)S(1)} %get-tuple-element.601, f32[8192,16]{1,0:T(8,128)} %copy.139, f32[]{:T(128)} %constant.96.clone.1), kind=kCustom, calls=%fused_computation.168 | custom fusion | bytes 524800 | tf_op jit(solution)/shard_map/scatter | solution.py:136
  404.7 3.5 copy.140
  (548 shorter events, 213.6 us)
Async XLA Ops:
  0.0 38.1 %copy-start = (f32[16,64,512]{2,1,0:T(8,128)S(1)}, f32[16,64,512]{2,1,0:T(8,128)}, u32[]{:S(2)}) copy-start(f32[16,64,512]{2,1,0:T(8,128)} %param.44) | copy-start | bytes 6291460
  35.1 4.9 %copy-start.7 = (f32[16,64,64]{2,1,0:T(8,128)S(1)}, f32[16,64,64]{2,1,0:T(8,128)}, u32[]{:S(2)}) copy-start(f32[16,64,64]{2,1,0:T(8,128)} %param.45) | copy-start | bytes 786436
  35.1 5.3 %copy-start.11 = (f32[1,64,64]{2,1,0:T(8,128)S(1)}, f32[1,64,64]{2,1,0:T(8,128)}, u32[]{:S(2)}) copy-start(f32[1,64,64]{2,1,0:T(8,128)} %param.46) | copy-start | bytes 49156
  35.1 5.5 %copy-start.15 = (f32[1,2,64]{2,1,0:T(2,128)S(1)}, f32[1,2,64]{2,1,0:T(2,128)}, u32[]{:S(2)}) copy-start(f32[1,2,64]{2,1,0:T(2,128)} %param.49) | copy-start | bytes 1540
  35.1 5.5 %copy-start.16 = (f32[1,2,64]{2,1,0:T(2,128)S(1)}, f32[1,2,64]{2,1,0:T(2,128)}, u32[]{:S(2)}) copy-start(f32[1,2,64]{2,1,0:T(2,128)} %param.48) | copy-start | bytes 1540
  35.1 15.5 %copy-start.13 = (f32[16,2,64]{2,1,0:T(2,128)S(1)}, f32[16,2,64]{2,1,0:T(2,128)}, u32[]{:S(2)}) copy-start(f32[16,2,64]{2,1,0:T(2,128)} %param.47) | copy-start | bytes 24580
  38.0 22.6 %copy-start.1 = (f32[3,3]{1,0:T(4,128)S(1)}, f32[3,3]{1,0:T(4,128)}, u32[]{:S(2)}) copy-start(f32[3,3]{1,0:T(4,128)} %constant.150.clone) | copy-start | bytes 112
  38.0 23.4 %copy-start.2 = (f32[3,3]{1,0:T(4,128)S(1)}, f32[3,3]{1,0:T(4,128)}, u32[]{:S(2)}) copy-start(f32[3,3]{1,0:T(4,128)} %constant.151.clone) | copy-start | bytes 112
  38.1 2.3 copy-start.9
  38.2 23.9 %copy-start.3 = (f32[3,3]{1,0:T(4,128)S(1)}, f32[3,3]{1,0:T(4,128)}, u32[]{:S(2)}) copy-start(f32[3,3]{1,0:T(4,128)} %constant.152.clone) | copy-start | bytes 112
  38.2 25.5 %copy-start.4 = (f32[3,3]{1,0:T(4,128)S(1)}, f32[3,3]{1,0:T(4,128)}, u32[]{:S(2)}) copy-start(f32[3,3]{1,0:T(4,128)} %constant.155.clone) | copy-start | bytes 112
  38.2 26.9 %copy-start.5 = (f32[3,3]{1,0:T(4,128)S(1)}, f32[3,3]{1,0:T(4,128)}, u32[]{:S(2)}) copy-start(f32[3,3]{1,0:T(4,128)} %constant.153.clone) | copy-start | bytes 112
  38.2 27.5 %copy-start.6 = (f32[3,3]{1,0:T(4,128)S(1)}, f32[3,3]{1,0:T(4,128)}, u32[]{:S(2)}) copy-start(f32[3,3]{1,0:T(4,128)} %constant.154.clone) | copy-start | bytes 112
  38.2 28.1 %copy-start.26 = (s32[1,8]{1,0:T(1,128)S(1)}, s32[1,8]{1,0:T(1,128)}, u32[]{:S(2)}) copy-start(s32[1,8]{1,0:T(1,128)} %param.52) | copy-start | bytes 100
  40.1 28.2 %copy-start.14 = (s32[16,16]{1,0:T(8,128)S(1)}, s32[16,16]{1,0:T(8,128)}, u32[]{:S(2)}) copy-start(s32[16,16]{1,0:T(8,128)} %param.50) | copy-start | bytes 3076
  40.1 28.3 %copy-start.27 = (s32[16]{0:T(128)S(1)}, s32[16]{0:T(128)}, u32[]{:S(2)}) copy-start(s32[16]{0:T(128)} %param.51) | copy-start | bytes 196
  41.5 329.0 %all-to-all-start = ((f32[32,18,128]{2,1,0:T(8,128)}), f32[32,18,128]{2,1,0:T(8,128)S(1)}, u32[]{:S(2)}, u32[]{:S(2)}) async-start(f32[32,18,128]{2,1,0:T(8,128)} %broadcast_in_dim.891), calls=%async_computation | async-start | bytes 786432 | tf_op jit(solution)/shard_map/all_to_all | solution.py:98
  69.1 70.8 %copy-start.12 = (f32[2,8192]{1,0:T(2,128)S(1)}, f32[2,8192]{1,0:T(2,128)}, u32[]{:S(2)}) copy-start(f32[2,8192]{1,0:T(2,128)} %param.42) | copy-start | bytes 196612
  139.9 35.4 %copy-start.10 = (f32[16,16,64]{2,1,0:T(8,128)}, f32[16,16,64]{2,1,0:T(8,128)S(1)}, u32[]{:S(2)}) copy-start(f32[16,16,64]{2,1,0:T(8,128)S(1)} %get-tuple-element.280) | copy-start | bytes 196612
  175.3 194.2 %copy-start.23 = (f32[64]{0:T(128)S(1)}, f32[64]{0:T(128)}, u32[]{:S(2)}) copy-start(f32[64]{0:T(128)} %get-tuple-element.505) | copy-start | bytes 772
  175.4 194.2 %copy-start.24 = (f32[64]{0:T(128)S(1)}, f32[64]{0:T(128)}, u32[]{:S(2)}) copy-start(f32[64]{0:T(128)} %get-tuple-element.506) | copy-start | bytes 772
  175.4 194.2 %copy-start.25 = (f32[64]{0:T(128)S(1)}, f32[64]{0:T(128)}, u32[]{:S(2)}) copy-start(f32[64]{0:T(128)} %get-tuple-element.507) | copy-start | bytes 772
  175.4 194.3 %copy-start.17 = (f32[64]{0:T(128)S(1)}, f32[64]{0:T(128)}, u32[]{:S(2)}) copy-start(f32[64]{0:T(128)} %get-tuple-element.496) | copy-start | bytes 772
  175.4 194.3 %copy-start.18 = (f32[64]{0:T(128)S(1)}, f32[64]{0:T(128)}, u32[]{:S(2)}) copy-start(f32[64]{0:T(128)} %get-tuple-element.497) | copy-start | bytes 772
  175.4 194.3 %copy-start.19 = (f32[64]{0:T(128)S(1)}, f32[64]{0:T(128)}, u32[]{:S(2)}) copy-start(f32[64]{0:T(128)} %get-tuple-element.498) | copy-start | bytes 772
  175.4 194.3 %copy-start.20 = (f32[64]{0:T(128)S(1)}, f32[64]{0:T(128)}, u32[]{:S(2)}) copy-start(f32[64]{0:T(128)} %get-tuple-element.618) | copy-start | bytes 772
  175.4 194.3 %copy-start.21 = (f32[64]{0:T(128)S(1)}, f32[64]{0:T(128)}, u32[]{:S(2)}) copy-start(f32[64]{0:T(128)} %get-tuple-element.619) | copy-start | bytes 772
  175.4 194.3 %copy-start.22 = (f32[64]{0:T(128)S(1)}, f32[64]{0:T(128)}, u32[]{:S(2)}) copy-start(f32[64]{0:T(128)} %get-tuple-element.620) | copy-start | bytes 772
  369.2 5.4 %copy-start.8 = (f32[16,64,64]{2,1,0:T(8,128)S(1)}, f32[16,64,64]{2,1,0:T(8,128)}, u32[]{:S(2)}) copy-start(f32[16,64,64]{2,1,0:T(8,128)} %param.45) | copy-start | bytes 786436

commit v3 on v2

v3 whole, which is shorter than its diff:
```python
import math

import jax
import jax.numpy as jnp
import numpy as np
from jax import lax
from jax.experimental import pallas as pl
from jax.experimental.pallas import tpu as pltpu
from jax.sharding import PartitionSpec as P

F32 = jnp.float32
BF16 = jnp.bfloat16
WIDE = 256
SHIFT = 8
LOG2E = math.log2(math.e)
TINY = 1e-37
PACK_ROWS = 24


def make_tables(norm):
    smooth = [0, 2, 4]
    sigmas = [1.0, 0.8, 1.2]
    rho = [[1.0, 0.5, 0.3], [0.5, 1.0, 0.4], [0.3, 0.4, 1.0]]
    scale = np.zeros((3, 3))
    poly = np.zeros((5, 3, 3))
    for first in range(3):
        for second in range(3):
            order = (smooth[first] + smooth[second]) // 2
            scale[first, second] = -(2.0 * order + 1.0) * (LOG2E / 0.3) ** 2
            amp = sigmas[first] * sigmas[second] * rho[first][second] * norm
            for power in range(order + 1):
                kterm = order - power
                coeff = math.factorial(order) / math.factorial(2 * order)
                coeff = (
                    coeff
                    * math.factorial(order + kterm)
                    / (math.factorial(kterm) * math.factorial(order - kterm))
                )
                poly[power, first, second] = amp * coeff * 2.0**power * (-1.0 / LOG2E) ** power
    return scale, poly


def dot(one, two, turned=False):
    dims = (((1,), (1 if turned else 0,)), ((), ()))
    return lax.dot_general(one, two, dims, preferred_element_type=F32)


def parts(value):
    high = value.astype(BF16)
    return high, (value - high.astype(F32)).astype(BF16)


def product(one, two, turned=False):
    rows = one.shape[0]
    one_hi, one_lo = parts(one)
    two_hi, two_lo = parts(two)
    both = dot(jnp.concatenate([one_hi, one_lo], axis=0), two_hi, turned)
    return both[:rows] + both[rows:] + dot(one_hi, two_lo, turned)


def one_hot(low):
    rows = lax.broadcasted_iota(jnp.int32, (WIDE, low.shape[1]), 0)
    return jnp.where(rows == low, 1.0, 0.0).astype(BF16)


def fill(source, value, at, nvec):
    high, low = parts(value)
    source[pl.ds(at, nvec), :WIDE] = high
    source[pl.ds(at, nvec), WIDE:] = low


def pick(source, index, nvec):
    count = index.shape[1]
    hot = one_hot(index & (WIDE - 1))
    hot = jnp.concatenate([hot, hot], axis=0)
    chunk = jnp.broadcast_to(index >> SHIFT, (8, count))[None]
    out = jnp.zeros((nvec // 8, 8, count), F32)
    chunks = source.shape[0] // nvec
    step = 4
    for first in range(0, chunks, step):
        found = dot(source[first * nvec : (first + step) * nvec, :], hot)
        found = found.reshape(step, nvec // 8, 8, count)
        for each in range(step):
            out = jnp.where(chunk == first + each, found[each], out)
    return out.reshape(nvec, count)


def up_kernel(
    vec, perm, bases, leaf_maps, node_maps, leaf_skel, node_skel, sub_skel, tree_vec, leaf_pack, tree_pack, source
):
    leaves, nvec, block = tree_vec.shape
    for each in range(vec.shape[1] // WIDE):
        fill(source, vec[:, each * WIDE : (each + 1) * WIDE], each * nvec, nvec)

    def gather(leaf, carry):
        tree_vec[leaf] = pick(source, perm[pl.ds(leaf, 1), :], nvec)
        return carry

    lax.fori_loop(0, leaves, gather, 0)
    rank = bases.shape[1]
    up_node = jnp.zeros((nvec, rank), F32)
    blank = jnp.zeros((PACK_ROWS - nvec - 2, 2 * rank), F32)
    for leaf in range(leaves):
        up = product(tree_vec[leaf], bases[leaf], True)
        skel = leaf_skel[leaf]
        twice = jnp.concatenate(
            [
                jnp.concatenate([up, up], axis=1),
                jnp.concatenate([skel, skel], axis=1),
                blank,
            ],
            axis=0,
        )
        for each in range(leaf_pack.shape[0]):
            leaf_pack[each, leaf] = twice
        up_node = up_node + product(up, leaf_maps[leaf])
    up_sub = product(up_node, node_maps[0])
    packed = jnp.concatenate(
        [
            jnp.concatenate([up_node, up_sub], axis=1),
            jnp.concatenate([node_skel[0], sub_skel[0]], axis=1),
            blank,
        ],
        axis=0,
    )

    def spread(each, carry):
        tree_pack[each] = packed
        return carry

    lax.fori_loop(0, tree_pack.shape[0], spread, 0)


def near_kernel(shift, tree_vec, crd, perm, near, inverse, flat, source, across, down, slots):
    leaves, nvec, block = tree_vec.shape
    chunks = crd.shape[1] // WIDE
    scale, poly = make_tables(1.0 / math.sqrt(block))
    slope = scale[0, 1] - scale[0, 0]
    for axis in range(2):
        for each in range(chunks):
            row = axis * chunks + each
            flat[row : row + 1, :] = crd[axis : axis + 1, each * WIDE : (each + 1) * WIDE]
    rest = flat[...]
    for piece in range(3):
        rounded = rest.astype(BF16)
        source[:, piece * WIDE : (piece + 1) * WIDE] = rounded
        rest = rest - rounded.astype(F32)
    slots[...] = jnp.zeros_like(slots)
    side = 128
    tiles = block // side

    def one_leaf(leaf, carry):
        index = perm[pl.ds(leaf, 1), :]
        hot = one_hot(index & (WIDE - 1))
        found = (
            dot(source[:, :WIDE], hot)
            + dot(source[:, WIDE : 2 * WIDE], hot)
            + dot(source[:, 2 * WIDE :], hot)
        )
        mine = lax.broadcasted_iota(jnp.int32, (chunks, block), 0) == index >> SHIFT
        lane = lax.broadcasted_iota(jnp.int32, (chunks, block), 1) + leaf * block
        lane_low = (lane % WIDE).astype(F32)
        lane_high = (lane // WIDE).astype(F32)
        marks = jnp.concatenate(
            [jnp.where(mine, lane_low, 0.0), jnp.where(mine, lane_high, 0.0)], axis=0
        ).astype(BF16)
        slots[...] += dot(marks, hot, True)
        row_x = jnp.sum(jnp.where(mine, found[:chunks], 0.0), axis=0, keepdims=True)
        row_y = jnp.sum(jnp.where(mine, found[chunks:], 0.0), axis=0, keepdims=True)
        moved = index + shift[0]
        kind = moved - 3 * ((moved * 43691) >> 17)
        row_w = kind.astype(F32) * slope
        for place, row in enumerate((row_x, row_y, row_w)):
            turned = jnp.transpose(jnp.broadcast_to(row, (side, block)))
            down[place] = turned.reshape(block // 8, 8, side)
        wide_kind = jnp.broadcast_to(kind, (8, block))
        is_zero, is_one = wide_kind == 0, wide_kind == 1
        across[0] = jnp.broadcast_to(row_x, (8, block))
        across[1] = jnp.broadcast_to(row_y, (8, block))
        across[2] = jnp.broadcast_to(row_w, (8, block)) + scale[0, 0]
        for power in range(5):
            for first in range(3):
                across[3 + power * 3 + first] = jnp.where(
                    is_zero,
                    poly[power, first, 0],
                    jnp.where(is_one, poly[power, first, 1], poly[power, first, 2]),
                )
        vec_hi, vec_lo = parts(tree_vec[leaf])
        vec_both = jnp.concatenate([vec_hi, vec_lo], axis=0)
        total = [None] * tiles
        for col in range(tiles):
            cols = slice(col * side, (col + 1) * side)
            table = [across[each, :, cols][None] for each in range(18)]
            high, low = [], []
            for row in range(col + 1):
                rows = slice(row * side // 8, (row + 1) * side // 8)
                diff_x = down[0, rows] - table[0]
                diff_y = down[1, rows] - table[1]
                down_w = down[2, rows]
                var_zero, var_one = down_w > 0.5 * slope, down_w > 1.5 * slope
                square = (diff_x * diff_x + diff_y * diff_y) * (down_w + table[2])
                arg = square * lax.rsqrt(TINY - square)

                def lookup(power):
                    a, b, c = table[3 + power * 3 : 6 + power * 3]
                    return jnp.where(var_zero, a, jnp.where(var_one, b, c))

                value = lookup(4)
                for power in (3, 2, 1, 0):
                    value = value * arg + lookup(power)
                value = (value * jnp.exp2(arg)).reshape(side, side)
                value_hi, value_lo = parts(value)
                high.append(value_hi)
                low.append(value_lo)
            high = jnp.concatenate(high, axis=0)
            low = jnp.concatenate(low, axis=0)
            upto = (col + 1) * side
            both = dot(vec_both[:, :upto], high)
            total[col] = both[:nvec] + both[nvec:] + dot(vec_hi[:, :upto], low)
            if col > 0:
                both = dot(vec_both[:, cols], high[: col * side], True)
                back = both[:nvec] + both[nvec:] + dot(vec_hi[:, cols], low[: col * side], True)
                for row in range(col):
                    total[row] = total[row] + back[:, row * side : (row + 1) * side]
        for col in range(tiles):
            near[leaf, :, col * side : (col + 1) * side] = total[col]
        return carry

    lax.fori_loop(0, leaves, one_leaf, 0)
    inverse[...] = (slots[:chunks] + slots[chunks:] * WIDE).astype(jnp.int32)


def far_kernel(
    place,
    leaf_src,
    leaf_count,
    node_src,
    node_count,
    leaf_all,
    tree_all,
    leaf_skel,
    node_skel,
    sub_skel,
    near,
    inverse,
    bases,
    leaf_maps,
    node_maps,
    tables,
    out,
    source,
    coef,
    subs,
):
    leaves, nvec, block = near.shape
    rank = bases.shape[1]
    subtrees = subs.shape[0]
    groups = tree_all.shape[0] // subtrees
    sub_pos = place[0]
    left = lax.broadcasted_iota(jnp.int32, (PACK_ROWS, 2 * rank), 1) < rank
    left_vec = lax.broadcasted_iota(jnp.int32, (nvec, 2 * rank), 1)

    def upright(row):
        return jnp.transpose(jnp.broadcast_to(row, (2 * rank, rank)))

    def term(packs, lives, col_x, col_y):
        row_x, row_y = packs[nvec : nvec + 1], packs[nvec + 1 : nvec + 2]
        diff_x, diff_y = col_x - row_x, col_y - row_y
        square = (diff_x * diff_x + diff_y * diff_y) * tables[0]
        arg = square * lax.rsqrt(TINY - square)
        value = tables[5]
        for power in (4, 3, 2, 1):
            value = value * arg + tables[power]
        value = value * jnp.exp2(arg)
        return product(jnp.where(lives, packs[:nvec], 0.0), value, True)

    def one_leaf(leaf, carry):
        count = leaf_count[leaf]
        skel = leaf_skel[leaf]
        col_x, col_y = upright(skel[0:1]), upright(skel[1:2])

        def pair(step, total):
            first = leaf_src[leaf, 2 * step]
            second = leaf_src[leaf, 2 * step + 1]
            packs = jnp.where(left, leaf_all[first], leaf_all[second])
            lives = left_vec < (count - 2 * step) * rank
            return total + term(packs, lives, col_x, col_y)

        coef[leaf] = lax.fori_loop(0, (count + 1) // 2, pair, jnp.zeros((nvec, rank), F32))
        return carry

    lax.fori_loop(0, leaves, one_leaf, 0)

    nodes = tree_all.shape[0]
    count = node_count[0]
    col_x, col_y = upright(node_skel[0, 0:1]), upright(node_skel[0, 1:2])
    base = (sub_pos - 1) * groups

    def node_pair(step, total):
        first = jnp.clip(node_src[0, 2 * step] + base, 0, nodes - 1)
        second = jnp.clip(node_src[0, 2 * step + 1] + base, 0, nodes - 1)
        packs = jnp.where(left, tree_all[first], pltpu.roll(tree_all[second], rank, 1))
        lives = left_vec < (count - 2 * step) * rank
        return total + term(packs, lives, col_x, col_y)

    down_node = lax.fori_loop(0, (count + 1) // 2, node_pair, jnp.zeros((nvec, rank), F32))

    def add_up(sub, carry):
        total = tree_all[sub * groups]
        for each in range(1, groups):
            total = total + tree_all[sub * groups + each]
        subs[sub, :nvec] = total[:nvec]
        subs[sub, nvec:] = tree_all[sub * groups, nvec:]
        return carry

    lax.fori_loop(0, subtrees, add_up, 0)
    col_x, col_y = upright(sub_skel[0, 0:1]), upright(sub_skel[0, 1:2])

    def sub_pair(step, total):
        first = 2 * step
        packs = jnp.where(left, pltpu.roll(subs[first], rank, 1), subs[first + 1])
        apart = jnp.abs(jnp.where(left_vec < rank, first, first + 1) - sub_pos)
        return total + term(packs, apart >= 2, col_x, col_y)

    far_sub = lax.fori_loop(0, subtrees // 2, sub_pair, jnp.zeros((nvec, rank), F32))
    down_node = down_node + product(far_sub, node_maps[0], True)
    for leaf in range(leaves):
        down_leaf = coef[leaf] + product(down_node, leaf_maps[leaf], True)
        rows = near[leaf] + product(down_leaf, bases[leaf])
        for each in range(block // WIDE):
            fill(
                source,
                rows[:, each * WIDE : (each + 1) * WIDE],
                (leaf * (block // WIDE) + each) * nvec,
                nvec,
            )

    def scatter(each, carry):
        at = pl.multiple_of(each * WIDE, WIDE)
        out[:, pl.ds(at, WIDE)] = pick(source, inverse[pl.ds(each, 1), :], nvec)
        return carry

    lax.fori_loop(0, inverse.shape[0], scatter, 0)


def skeleton_tables(rank):
    scale, poly = make_tables(1.0 / math.sqrt(rank))
    var = np.arange(rank) % 3
    rows, cols = var[:, None], np.tile(var, 2)[None, :]
    return np.stack([scale[rows, cols]] + [poly[power][rows, cols] for power in range(5)]).astype(
        np.float32
    )


def shards(
    vectors,
    coords,
    perm,
    bases,
    leaf_maps,
    node_maps,
    leaf_skel,
    node_skel,
    sub_skel,
    leaf_src,
    leaf_count,
    node_src,
    node_count,
):
    nvec, rows_dev = vectors.shape
    leaves, rank, block = bases.shape
    groups = lax.axis_size("grp")
    subtrees = lax.axis_size("leaf")
    nodes = groups * subtrees
    sub_pos = lax.axis_index("leaf")
    device_pos = sub_pos * groups + lax.axis_index("grp")
    chunks = rows_dev // WIDE
    vmem = pl.BlockSpec(memory_space=pltpu.VMEM)
    smem = pl.BlockSpec(memory_space=pltpu.SMEM)
    params = pltpu.CompilerParams(vmem_limit_bytes=48 * 1024 * 1024)
    order = perm.reshape(leaves, block)
    tree_vec, leaf_pack, tree_pack = pl.pallas_call(
        up_kernel,
        out_shape=(
            jax.ShapeDtypeStruct((leaves, nvec, block), F32),
            jax.ShapeDtypeStruct((groups, leaves, PACK_ROWS, 2 * rank), F32),
            jax.ShapeDtypeStruct((nodes, PACK_ROWS, 2 * rank), F32),
        ),
        in_specs=[vmem] * 8,
        out_specs=(vmem,) * 3,
        scratch_shapes=[pltpu.VMEM((chunks * nvec, 2 * WIDE), BF16)],
        compiler_params=params,
        name="up",
    )(vectors, order, bases, leaf_maps, node_maps, leaf_skel, node_skel, sub_skel)
    tree_all = lax.all_to_all(tree_pack, ("leaf", "grp"), 0, 0, tiled=True)
    leaf_all = lax.all_to_all(leaf_pack, "grp", 0, 0, tiled=True)
    shift = (device_pos * (rows_dev % 3) % 3).astype(jnp.int32).reshape(1)
    near, inverse = pl.pallas_call(
        near_kernel,
        out_shape=(
            jax.ShapeDtypeStruct((leaves, nvec, block), F32),
            jax.ShapeDtypeStruct((chunks, WIDE), jnp.int32),
        ),
        in_specs=[smem] + [vmem] * 3,
        out_specs=(vmem,) * 2,
        scratch_shapes=[
            pltpu.VMEM((2 * chunks, WIDE), F32),
            pltpu.VMEM((2 * chunks, 3 * WIDE), BF16),
            pltpu.VMEM((18, 8, block), F32),
            pltpu.VMEM((3, block // 8, 8, 128), F32),
            pltpu.VMEM((2 * chunks, WIDE), F32),
        ],
        compiler_params=params,
        cost_estimate=pl.CostEstimate(
            flops=2 * 16 * leaves * block * block * 4, bytes_accessed=4 * leaves * nvec * block * 2, transcendentals=leaves * block * block
        ),
        name="near",
    )(shift, tree_vec, coords, order)
    return pl.pallas_call(
        far_kernel,
        out_shape=jax.ShapeDtypeStruct((nvec, rows_dev), F32),
        in_specs=[smem] * 5 + [vmem] * 11,
        out_specs=vmem,
        scratch_shapes=[
            pltpu.VMEM((chunks * nvec, 2 * WIDE), BF16),
            pltpu.VMEM((leaves, nvec, rank), F32),
            pltpu.VMEM((subtrees, PACK_ROWS, 2 * rank), F32),
        ],
        compiler_params=params,
        name="far",
    )(
        sub_pos.astype(jnp.int32).reshape(1),
        leaf_src,
        leaf_count,
        node_src,
        node_count,
        leaf_all.reshape(groups * leaves, PACK_ROWS, 2 * rank),
        tree_all,
        leaf_skel,
        node_skel,
        sub_skel,
        near,
        inverse,
        bases,
        leaf_maps,
        node_maps,
        jnp.asarray(skeleton_tables(rank)),
    )


def solution(mesh):
    placed = (
        P(None, ("leaf", "grp")),
        P(None, ("leaf", "grp")),
        P(("leaf", "grp")),
        P(("leaf", "grp"), None, None),
        P(("leaf", "grp"), None, None),
        P(("leaf", "grp"), None, None),
        P(("leaf", "grp"), None, None),
        P(("leaf", "grp"), None, None),
        P("leaf", None, None),
        P(("leaf", "grp"), None),
        P(("leaf", "grp")),
        P(("leaf", "grp"), None),
        P(("leaf", "grp")),
    )
    return jax.shard_map(
        shards, mesh=mesh, in_specs=placed, out_specs=P(None, ("leaf", "grp")), check_vma=False
    )
```

time: 411 us -> 109 us (0.27)
  the two profiles are of different devices: /device:TPU:0 before, /device:TPU:23 now
where the time goes in v3:
time: 109 us; the launch traced here: 108 us
  Pallas kernels  75.4 us (69%)
  blocking collectives  13.2 us (12%)
  local copies, waits for them, and re-layouts  12 us (11%)
  starting transfers between devices  6.35 us (6%)
    pallas_call x1, Pallas kernels, shards(): pl.pallas_call(far_kernel, out_shape=jax.ShapeDtypeStruct((nvec, rows_dev...  36.5 us
    pallas_call x1, Pallas kernels, shards(): pl.pallas_call(near_kernel, out_shape=(jax.ShapeDtypeStruct((leaves, nvec...  21.3 us
    pallas_call x1, Pallas kernels, shards(): pl.pallas_call(up_kernel, out_shape=(jax.ShapeDtypeStruct((leaves, nvec,...  17.6 us
    all_to_all x1, blocking collectives, shards(): leaf_all = lax.all_to_all(leaf_pack, 'grp', 0, 0, tiled=True)  13.2 us
    unnamed x44, local copies, waits for them, and re-layouts  11.2 us
    all_to_all x1, starting transfers between devices, shards(): tree_all = lax.all_to_all(tree_pack, ('leaf', 'grp'), 0, 0, tiled=True)  6.35 us
  transfers between devices with their start and end apart: 1, of which 0 were waited for; matrix products, arithmetic and copies ran while one was open for 0% of the time, Pallas kernels for 20%

profile of v3, /device:TPU:23, one launch (start us, length us, event | category | flops | bytes accessed | tf_op | source)
XLA Modules:
  0.0 107.7 jit_solution(11846729415920870550)
XLA Ops:
  0.0 0.8 reshape.13.perm
  0.8 1.6 %copy-done = f32[16,64,512]{2,1,0:T(8,128)S(1)} copy-done((f32[16,64,512]{2,1,0:T(8,128)S(1)}, f32[16,64,512]{2,1,0:T(8,128)}, u32[]{:S(2)}) %copy-start) | copy-done | bytes 2097176
  2.4 1.0 copy-done.2
  3.4 1.0 copy-done.6
  4.4 0.8 copy-done.8
  5.2 0.7 copy-done.10
  5.9 0.7 copy-done.13
  6.6 0.7 copy-done.15
  7.3 17.6 %up.1 = (f32[16,16,512]{2,1,0:T(8,128)S(1)}, f32[4,16,24,128]{3,2,1,0:T(8,128)S(1)}, f32[32,24,128]{2,1,0:T(8,128)}) custom-call(f32[16,8192]{1,0:T(8,128)S(1)} %copy-done.6, s32[16,512]{1,0:T(8,128)S(1)} %reshape.13.perm, f32[16,64,512]{2,1,0:T(8,128)S(1)} %copy-done, f32[16,64,64]{2,1,0:T(8,128)S(1)} %copy-done.2, f32[1,64,64]{2,1,0:T(8,128)S(1)} %copy-done.8, ...), custom_call_target="tpu_custom_call" | custom-call | tf_op jit(solution)/shard_map/up/pallas_call | solution.py:382
  24.9 13.2 %all_to_all.10 = f32[4,16,24,128]{3,2,1,0:T(8,128)S(1)} all-to-all(f32[4,16,24,128]{3,2,1,0:T(8,128)S(1)} %get-tuple-element.10), channel_id=1, replica_groups=mesh['leaf'=8,'grp'=4] {'grp'}, dimensions={0} | all-to-all | bytes 1572864 | tf_op jit(solution)/shard_map/all_to_all | solution.py:396
  38.0 0.0 copy-done.19
  38.0 6.3 %all-to-all-start.1 = ((f32[32,24,128]{2,1,0:T(8,128)}), f32[32,24,128]{2,1,0:T(8,128)}, u32[]{:S(2)}, u32[]{:S(2)}) async-start(f32[32,24,128]{2,1,0:T(8,128)} %get-tuple-element.11), calls=%async_computation.1 | async-start | bytes 786432 | tf_op jit(solution)/shard_map/all_to_all | solution.py:395
  45.1 0.0 copy-start.20
  45.1 1.0 copy-done.20
  46.1 0.8 copy-done.21
  47.0 0.0 copy-start.12
  47.0 0.0 copy-start.14
  47.0 0.0 copy-start.16
  47.0 0.0 copy-start.17
  47.0 0.0 copy-start.18
  47.0 21.3 %near.1 = (f32[16,16,512]{2,1,0:T(8,128)S(1)}, s32[32,256]{1,0:T(8,128)S(1)}) custom-call(s32[1]{0:T(128)} %bitcast.2.shift, f32[16,16,512]{2,1,0:T(8,128)S(1)} %copy-done.20, f32[2,8192]{1,0:T(2,128)S(1)} %copy-done.21, s32[16,512]{1,0:T(8,128)S(1)} %reshape.13.perm), custom_call_target="tpu_custom_call" | custom-call | flops 536870912 | bytes 1048576 | tf_op jit(solution)/shard_map/near/pallas_call | solution.py:398
  68.3 0.8 copy-done.4
  69.1 0.0 all-to-all-done.1.tree_all
  69.1 0.0 copy-done.1
  69.1 0.0 copy-done.3
  69.2 0.0 copy-done.9
  69.2 0.0 copy-done.11
  69.2 0.0 copy-done.12
  69.2 0.0 copy-done.14
  69.2 1.0 copy-done.5
  70.3 0.9 copy-done.7
  71.2 36.5 %far.1 = f32[16,8192]{1,0:T(8,128)} custom-call(s32[1]{0:T(128)} %bitcast.place, s32[16,16]{1,0:T(8,128)S(1)} %copy-done.12, s32[16]{0:T(128)S(1)} %copy-done.17, s32[1,8]{1,0:T(1,128)S(1)} %copy-done.18, s32[1]{0:T(128)S(6)} %copy.15.node_count, f32[64,24,128]{2,1,0:T(8,128)S(1)} %bitcast.3, f32[32,24,128]{2,1,0:T(8,128)} %all-to-all-done.1.tree_all, ...), custom_call_target="tpu_custom_call" | custom-call | tf_op jit(solution)/shard_map/far/pallas_call | solution.py:419
  (19 shorter events, 0.0 us)
Async XLA Ops:
  0.8 1.6 %copy-start = (f32[16,64,512]{2,1,0:T(8,128)S(1)}, f32[16,64,512]{2,1,0:T(8,128)}, u32[]{:S(2)}) copy-start(f32[16,64,512]{2,1,0:T(8,128)} %bases.3) | copy-start | bytes 6291460
  2.4 1.0 copy-start.2
  3.4 1.0 copy-start.6
  4.4 0.8 copy-start.8
  5.2 0.7 copy-start.10
  5.9 0.7 copy-start.13
  6.6 0.7 copy-start.15
  24.9 13.2 %copy-start.19 = (f32[16,16,512]{2,1,0:T(8,128)}, f32[16,16,512]{2,1,0:T(8,128)S(1)}, u32[]{:S(2)}) copy-start(f32[16,16,512]{2,1,0:T(8,128)S(1)} %get-tuple-element.12.tree_vec) | copy-start | bytes 1572868
  38.0 31.1 %all-to-all-start.1 = ((f32[32,24,128]{2,1,0:T(8,128)}), f32[32,24,128]{2,1,0:T(8,128)}, u32[]{:S(2)}, u32[]{:S(2)}) async-start(f32[32,24,128]{2,1,0:T(8,128)} %get-tuple-element.11), calls=%async_computation.1 | async-start | bytes 786432 | tf_op jit(solution)/shard_map/all_to_all | solution.py:395
  45.1 1.0 copy-start.20
  46.1 0.8 copy-start.21
  47.0 22.2 %copy-start.1 = (f32[16,64,512]{2,1,0:T(8,128)S(1)}, f32[16,64,512]{2,1,0:T(8,128)}, u32[]{:S(2)}) copy-start(f32[16,64,512]{2,1,0:T(8,128)} %bases.3) | copy-start | bytes 6291460
  47.0 22.2 %copy-start.3 = (f32[16,64,64]{2,1,0:T(8,128)S(1)}, f32[16,64,64]{2,1,0:T(8,128)}, u32[]{:S(2)}) copy-start(f32[16,64,64]{2,1,0:T(8,128)} %leaf_maps.3) | copy-start | bytes 786436
  47.0 22.2 %copy-start.9 = (f32[1,64,64]{2,1,0:T(8,128)S(1)}, f32[1,64,64]{2,1,0:T(8,128)}, u32[]{:S(2)}) copy-start(f32[1,64,64]{2,1,0:T(8,128)} %node_maps.3) | copy-start | bytes 49156
  47.0 22.2 %copy-start.11 = (f32[16,2,64]{2,1,0:T(2,128)S(1)}, f32[16,2,64]{2,1,0:T(2,128)}, u32[]{:S(2)}) copy-start(f32[16,2,64]{2,1,0:T(2,128)} %leaf_skel.3) | copy-start | bytes 24580
  47.0 22.2 %copy-start.12 = (s32[16,16]{1,0:T(8,128)S(1)}, s32[16,16]{1,0:T(8,128)}, u32[]{:S(2)}) copy-start(s32[16,16]{1,0:T(8,128)} %leaf_src.1) | copy-start | bytes 3076
  47.0 22.2 %copy-start.14 = (f32[1,2,64]{2,1,0:T(2,128)S(1)}, f32[1,2,64]{2,1,0:T(2,128)}, u32[]{:S(2)}) copy-start(f32[1,2,64]{2,1,0:T(2,128)} %node_skel.3) | copy-start | bytes 1540
  47.0 22.2 %copy-start.16 = (f32[1,2,64]{2,1,0:T(2,128)S(1)}, f32[1,2,64]{2,1,0:T(2,128)}, u32[]{:S(2)}) copy-start(f32[1,2,64]{2,1,0:T(2,128)} %sub_skel.3) | copy-start | bytes 1540
  47.0 22.2 %copy-start.17 = (s32[16]{0:T(128)S(1)}, s32[16]{0:T(128)}, u32[]{:S(2)}) copy-start(s32[16]{0:T(128)} %leaf_count.1) | copy-start | bytes 196
  47.0 22.2 %copy-start.18 = (s32[1,8]{1,0:T(1,128)S(1)}, s32[1,8]{1,0:T(1,128)}, u32[]{:S(2)}) copy-start(s32[1,8]{1,0:T(1,128)} %node_src.1) | copy-start | bytes 100
  68.3 0.8 copy-start.4
  69.2 1.0 copy-start.5
  70.3 0.9 copy-start.7

commit v4 on v3

--- a/solution.py
+++ b/solution.py
@@ -1,3 +1,4 @@
+import functools
 import math
 
 import jax
@@ -15,6 +16,7 @@
 LOG2E = math.log2(math.e)
 TINY = 1e-37
 PACK_ROWS = 24
+AT_ONCE = 4
 
 
 def make_tables(norm):
@@ -76,44 +78,57 @@
     chunk = jnp.broadcast_to(index >> SHIFT, (8, count))[None]
     out = jnp.zeros((nvec // 8, 8, count), F32)
     chunks = source.shape[0] // nvec
-    step = 4
-    for first in range(0, chunks, step):
-        found = dot(source[first * nvec : (first + step) * nvec, :], hot)
-        found = found.reshape(step, nvec // 8, 8, count)
-        for each in range(step):
-            out = jnp.where(chunk == first + each, found[each], out)
+    found = dot(source[...], hot).reshape(chunks, nvec // 8, 8, count)
+    for each in range(chunks):
+        out = jnp.where(chunk == each, found[each], out)
     return out.reshape(nvec, count)
 
 
-def up_kernel(
-    vec, perm, bases, leaf_maps, node_maps, leaf_skel, node_skel, sub_skel, tree_vec, leaf_pack, tree_pack, source
-):
+def leaf_index(perm, leaf, block):
+    rows = block // 128
+    return jnp.concatenate([perm[pl.ds(leaf * rows + each, 1), :] for each in range(rows)], axis=1)
+
+
+def fetch(pairs, sems):
+    copies = [pltpu.make_async_copy(src, dst, sems.at[each]) for each, (src, dst) in enumerate(pairs)]
+    for copy in copies:
+        copy.start()
+    return copies
+
+
+def up_kernel(*refs):
+    given, (tree_vec, leaf_pack, tree_pack) = refs[:8], refs[8:11]
+    held, source, sems = refs[11:19], refs[19], refs[20]
+    copies = fetch(list(zip(given, held)), sems)
+    vec, perm, bases, leaf_maps, node_maps, leaf_skel, node_skel, sub_skel = held
     leaves, nvec, block = tree_vec.shape
+    rank = bases.shape[1]
+    copies[0].wait()
     for each in range(vec.shape[1] // WIDE):
         fill(source, vec[:, each * WIDE : (each + 1) * WIDE], each * nvec, nvec)
+    copies[1].wait()
 
     def gather(leaf, carry):
-        tree_vec[leaf] = pick(source, perm[pl.ds(leaf, 1), :], nvec)
+        tree_vec[leaf] = pick(source, leaf_index(perm, leaf, block), nvec)
         return carry
 
     lax.fori_loop(0, leaves, gather, 0)
-    rank = bases.shape[1]
+    for copy in copies[2:]:
+        copy.wait()
     up_node = jnp.zeros((nvec, rank), F32)
     blank = jnp.zeros((PACK_ROWS - nvec - 2, 2 * rank), F32)
-    for leaf in range(leaves):
-        up = product(tree_vec[leaf], bases[leaf], True)
-        skel = leaf_skel[leaf]
-        twice = jnp.concatenate(
+    for leaf in range(0, leaves, 2):
+        up = [product(tree_vec[leaf + each], bases[leaf + each], True) for each in range(2)]
+        leaf_pack[leaf // 2] = jnp.concatenate(
             [
-                jnp.concatenate([up, up], axis=1),
-                jnp.concatenate([skel, skel], axis=1),
+                jnp.concatenate(up, axis=1),
+                jnp.concatenate([leaf_skel[leaf], leaf_skel[leaf + 1]], axis=1),
                 blank,
             ],
             axis=0,
         )
-        for each in range(leaf_pack.shape[0]):
-            leaf_pack[each, leaf] = twice
-        up_node = up_node + product(up, leaf_maps[leaf])
+        for each in range(2):
+            up_node = up_node + product(up[each], leaf_maps[leaf + each])
     up_sub = product(up_node, node_maps[0])
     packed = jnp.concatenate(
         [
@@ -131,7 +146,12 @@
     lax.fori_loop(0, tree_pack.shape[0], spread, 0)
 
 
-def near_kernel(shift, tree_vec, crd, perm, near, inverse, flat, source, across, down, slots):
+def near_kernel(
+    shift, tree_vec, crd_in, perm_in, near, inverse, crd, perm, flat, source, across, down, slots, sems
+):
+    copies = fetch([(crd_in, crd), (perm_in, perm)], sems)
+    for copy in copies:
+        copy.wait()
     leaves, nvec, block = tree_vec.shape
     chunks = crd.shape[1] // WIDE
     scale, poly = make_tables(1.0 / math.sqrt(block))
@@ -150,7 +170,7 @@
     tiles = block // side
 
     def one_leaf(leaf, carry):
-        index = perm[pl.ds(leaf, 1), :]
+        index = leaf_index(perm, leaf, block)
         hot = one_hot(index & (WIDE - 1))
         found = (
             dot(source[:, :WIDE], hot)
@@ -230,100 +250,131 @@
     inverse[...] = (slots[:chunks] + slots[chunks:] * WIDE).astype(jnp.int32)
 
 
-def far_kernel(
-    place,
-    leaf_src,
-    leaf_count,
-    node_src,
-    node_count,
-    leaf_all,
-    tree_all,
-    leaf_skel,
-    node_skel,
-    sub_skel,
-    near,
-    inverse,
-    bases,
-    leaf_maps,
-    node_maps,
-    tables,
-    out,
-    source,
-    coef,
-    subs,
-):
+def far_kernel(groups, subtrees, *refs):
+    place, leaf_src, leaf_count, node_src, node_count, leaf_all, tree_all, near, inverse = refs[:9]
+    given, out = refs[9:16], refs[16]
+    held = refs[17:24]
+    source, coef, twice, cols, srcs, dsts, sems = refs[24:]
+    copies = fetch(list(zip(given, held)), sems)
+    leaf_skel, node_skel, sub_skel, tables, leaf_maps, node_maps, bases = held
     leaves, nvec, block = near.shape
     rank = bases.shape[1]
-    subtrees = subs.shape[0]
-    groups = tree_all.shape[0] // subtrees
+    nodes = tree_all.shape[0]
+    pairs = leaf_all.shape[0]
+    node_at = 2 * pairs
+    beside = 3 * groups
+    sub_at = node_at + beside
+    blank = sub_at + subtrees
     sub_pos = place[0]
     left = lax.broadcasted_iota(jnp.int32, (PACK_ROWS, 2 * rank), 1) < rank
-    left_vec = lax.broadcasted_iota(jnp.int32, (nvec, 2 * rank), 1)
-
-    def upright(row):
-        return jnp.transpose(jnp.broadcast_to(row, (2 * rank, rank)))
-
-    def term(packs, lives, col_x, col_y):
-        row_x, row_y = packs[nvec : nvec + 1], packs[nvec + 1 : nvec + 2]
-        diff_x, diff_y = col_x - row_x, col_y - row_y
-        square = (diff_x * diff_x + diff_y * diff_y) * tables[0]
-        arg = square * lax.rsqrt(TINY - square)
-        value = tables[5]
-        for power in (4, 3, 2, 1):
-            value = value * arg + tables[power]
-        value = value * jnp.exp2(arg)
-        return product(jnp.where(lives, packs[:nvec], 0.0), value, True)
-
-    def one_leaf(leaf, carry):
+
+    def list_leaf(leaf, at):
         count = leaf_count[leaf]
-        skel = leaf_skel[leaf]
-        col_x, col_y = upright(skel[0:1]), upright(skel[1:2])
-
-        def pair(step, total):
-            first = leaf_src[leaf, 2 * step]
-            second = leaf_src[leaf, 2 * step + 1]
-            packs = jnp.where(left, leaf_all[first], leaf_all[second])
-            lives = left_vec < (count - 2 * step) * rank
-            return total + term(packs, lives, col_x, col_y)
-
-        coef[leaf] = lax.fori_loop(0, (count + 1) // 2, pair, jnp.zeros((nvec, rank), F32))
-        return carry
-
-    lax.fori_loop(0, leaves, one_leaf, 0)
-
-    nodes = tree_all.shape[0]
+
+        def one(step, carry):
+            srcs[2 * (at + step)] = leaf_src[leaf, 2 * step]
+            second = jnp.where(2 * step + 1 < count, leaf_src[leaf, 2 * step + 1], blank)
+            srcs[2 * (at + step) + 1] = second
+            dsts[at + step] = leaf
+            return carry
+
+        steps = (count + 1) // 2
+        lax.fori_loop(0, steps, one, 0)
+        return at + steps
+
+    size = lax.fori_loop(0, leaves, list_leaf, 0)
     count = node_count[0]
-    col_x, col_y = upright(node_skel[0, 0:1]), upright(node_skel[0, 1:2])
-    base = (sub_pos - 1) * groups
-
-    def node_pair(step, total):
-        first = jnp.clip(node_src[0, 2 * step] + base, 0, nodes - 1)
-        second = jnp.clip(node_src[0, 2 * step + 1] + base, 0, nodes - 1)
-        packs = jnp.where(left, tree_all[first], pltpu.roll(tree_all[second], rank, 1))
-        lives = left_vec < (count - 2 * step) * rank
-        return total + term(packs, lives, col_x, col_y)
-
-    down_node = lax.fori_loop(0, (count + 1) // 2, node_pair, jnp.zeros((nvec, rank), F32))
-
-    def add_up(sub, carry):
-        total = tree_all[sub * groups]
+
+    def list_node(step, carry):
+        srcs[2 * (size + step)] = node_at + node_src[0, 2 * step]
+        second = jnp.where(2 * step + 1 < count, node_at + node_src[0, 2 * step + 1], blank)
+        srcs[2 * (size + step) + 1] = second
+        dsts[size + step] = leaves
+        return carry
+
+    steps = (count + 1) // 2
+    lax.fori_loop(0, steps, list_node, 0)
+
+    def list_sub(sub, at):
+        srcs[at] = sub_at + sub
+        dsts[at // 2] = leaves + 1
+        return at + jnp.where(jnp.abs(sub - sub_pos) >= 2, 1, 0)
+
+    ends = lax.fori_loop(0, subtrees, list_sub, 2 * (size + steps))
+    srcs[ends] = blank
+    dsts[ends // 2] = leaves + 1
+    ends = (ends + 1) // 2
+    for each in range(AT_ONCE):
+        srcs[2 * (ends + each)] = blank
+        srcs[2 * (ends + each) + 1] = blank
+        dsts[ends + each] = leaves + 1
+
+    def both_leaves(pair, carry):
+        packs = leaf_all[pair]
+        turned = pltpu.roll(packs, rank, 1)
+        twice[2 * pair] = jnp.where(left, packs, turned)
+        twice[2 * pair + 1] = jnp.where(left, turned, packs)
+        return carry
+
+    lax.fori_loop(0, pairs, both_leaves, 0)
+
+    def both_node(each, carry):
+        packs = tree_all[jnp.clip((sub_pos - 1) * groups + each, 0, nodes - 1)]
+        twice[node_at + each] = jnp.where(left, packs, pltpu.roll(packs, rank, 1))
+        return carry
+
+    lax.fori_loop(0, beside, both_node, 0)
+
+    def both_sub(sub, carry):
+        total = tree_all[sub * groups, :nvec]
         for each in range(1, groups):
-            total = total + tree_all[sub * groups + each]
-        subs[sub, :nvec] = total[:nvec]
-        subs[sub, nvec:] = tree_all[sub * groups, nvec:]
-        return carry
-
-    lax.fori_loop(0, subtrees, add_up, 0)
-    col_x, col_y = upright(sub_skel[0, 0:1]), upright(sub_skel[0, 1:2])
-
-    def sub_pair(step, total):
-        first = 2 * step
-        packs = jnp.where(left, pltpu.roll(subs[first], rank, 1), subs[first + 1])
-        apart = jnp.abs(jnp.where(left_vec < rank, first, first + 1) - sub_pos)
-        return total + term(packs, apart >= 2, col_x, col_y)
-
-    far_sub = lax.fori_loop(0, subtrees // 2, sub_pair, jnp.zeros((nvec, rank), F32))
-    down_node = down_node + product(far_sub, node_maps[0], True)
+            total = total + tree_all[sub * groups + each, :nvec]
+        packs = jnp.concatenate([total, tree_all[sub * groups, nvec:]], axis=0)
+        twice[sub_at + sub] = jnp.where(left, pltpu.roll(packs, rank, 1), packs)
+        return carry
+
+    lax.fori_loop(0, subtrees, both_sub, 0)
+    twice[blank] = jnp.zeros_like(twice[blank])
+    coef[...] = jnp.zeros_like(coef)
+    for copy in copies[:4]:
+        copy.wait()
+
+    def upright(skel, at):
+        for axis in range(2):
+            row = jnp.broadcast_to(skel[axis : axis + 1], (2 * rank, rank))
+            cols[at, axis] = jnp.transpose(row)
+
+    def upright_leaf(leaf, carry):
+        upright(leaf_skel[leaf], leaf)
+        return carry
+
+    lax.fori_loop(0, leaves, upright_leaf, 0)
+    upright(node_skel[0], leaves)
+    upright(sub_skel[0], leaves + 1)
+
+    def couple(step, carry):
+        terms = []
+        for each in range(AT_ONCE):
+            item = step * AT_ONCE + each
+            packs = jnp.where(left, twice[srcs[2 * item]], twice[srcs[2 * item + 1]])
+            target = dsts[item]
+            diff_x = cols[target, 0] - packs[nvec : nvec + 1]
+            diff_y = cols[target, 1] - packs[nvec + 1 : nvec + 2]
+            square = (diff_x * diff_x + diff_y * diff_y) * tables[0]
+            arg = square * lax.rsqrt(TINY - square)
+            value = tables[5]
+            for power in (4, 3, 2, 1):
+                value = value * arg + tables[power]
+            value = value * jnp.exp2(arg)
+            terms.append((target, product(packs[:nvec], value, True)))
+        for target, total in terms:
+            coef[target] += total
+        return carry
+
+    lax.fori_loop(0, (ends + AT_ONCE - 1) // AT_ONCE, couple, 0)
+    for copy in copies[4:]:
+        copy.wait()
+    down_node = coef[leaves] + product(coef[leaves + 1], node_maps[0], True)
     for leaf in range(leaves):
         down_leaf = coef[leaf] + product(down_node, leaf_maps[leaf], True)
         rows = near[leaf] + product(down_leaf, bases[leaf])
@@ -336,11 +387,14 @@
             )
 
     def scatter(each, carry):
-        at = pl.multiple_of(each * WIDE, WIDE)
-        out[:, pl.ds(at, WIDE)] = pick(source, inverse[pl.ds(each, 1), :], nvec)
-        return carry
-
-    lax.fori_loop(0, inverse.shape[0], scatter, 0)
+        at = pl.multiple_of(each * 2 * WIDE, 2 * WIDE)
+        index = jnp.concatenate(
+            [inverse[pl.ds(2 * each, 1), :], inverse[pl.ds(2 * each + 1, 1), :]], axis=1
+        )
+        out[:, pl.ds(at, 2 * WIDE)] = pick(source, index, nvec)
+        return carry
+
+    lax.fori_loop(0, inverse.shape[0] // 2, scatter, 0)
 
 
 def skeleton_tables(rank):
@@ -377,23 +431,30 @@
     chunks = rows_dev // WIDE
     vmem = pl.BlockSpec(memory_space=pltpu.VMEM)
     smem = pl.BlockSpec(memory_space=pltpu.SMEM)
-    params = pltpu.CompilerParams(vmem_limit_bytes=48 * 1024 * 1024)
-    order = perm.reshape(leaves, block)
+    hbm = pl.BlockSpec(memory_space=pl.ANY)
+    params = pltpu.CompilerParams(vmem_limit_bytes=20 * 1024 * 1024)
+    order = perm.reshape(rows_dev // 128, 128)
+
+    def like(*arrays):
+        return [pltpu.VMEM(each.shape, each.dtype) for each in arrays]
+
+    given = (vectors, order, bases, leaf_maps, node_maps, leaf_skel, node_skel, sub_skel)
     tree_vec, leaf_pack, tree_pack = pl.pallas_call(
         up_kernel,
         out_shape=(
             jax.ShapeDtypeStruct((leaves, nvec, block), F32),
-            jax.ShapeDtypeStruct((groups, leaves, PACK_ROWS, 2 * rank), F32),
+            jax.ShapeDtypeStruct((leaves // 2, PACK_ROWS, 2 * rank), F32),
             jax.ShapeDtypeStruct((nodes, PACK_ROWS, 2 * rank), F32),
         ),
-        in_specs=[vmem] * 8,
+        in_specs=[hbm] * 8,
         out_specs=(vmem,) * 3,
-        scratch_shapes=[pltpu.VMEM((chunks * nvec, 2 * WIDE), BF16)],
+        scratch_shapes=like(*given)
+        + [pltpu.VMEM((chunks * nvec, 2 * WIDE), BF16), pltpu.SemaphoreType.DMA((8,))],
         compiler_params=params,
         name="up",
-    )(vectors, order, bases, leaf_maps, node_maps, leaf_skel, node_skel, sub_skel)
+    )(*given)
     tree_all = lax.all_to_all(tree_pack, ("leaf", "grp"), 0, 0, tiled=True)
-    leaf_all = lax.all_to_all(leaf_pack, "grp", 0, 0, tiled=True)
+    leaf_all = lax.all_gather(leaf_pack, "grp", axis=0, tiled=True)
     shift = (device_pos * (rows_dev % 3) % 3).astype(jnp.int32).reshape(1)
     near, inverse = pl.pallas_call(
         near_kernel,
@@ -401,30 +462,42 @@
             jax.ShapeDtypeStruct((leaves, nvec, block), F32),
             jax.ShapeDtypeStruct((chunks, WIDE), jnp.int32),
         ),
-        in_specs=[smem] + [vmem] * 3,
+        in_specs=[smem, vmem, hbm, hbm],
         out_specs=(vmem,) * 2,
-        scratch_shapes=[
+        scratch_shapes=like(coords, order)
+        + [
             pltpu.VMEM((2 * chunks, WIDE), F32),
             pltpu.VMEM((2 * chunks, 3 * WIDE), BF16),
             pltpu.VMEM((18, 8, block), F32),
             pltpu.VMEM((3, block // 8, 8, 128), F32),
             pltpu.VMEM((2 * chunks, WIDE), F32),
+            pltpu.SemaphoreType.DMA((2,)),
         ],
         compiler_params=params,
         cost_estimate=pl.CostEstimate(
-            flops=2 * 16 * leaves * block * block * 4, bytes_accessed=4 * leaves * nvec * block * 2, transcendentals=leaves * block * block
+            flops=128 * leaves * block * block,
+            bytes_accessed=8 * leaves * nvec * block,
+            transcendentals=leaves * block * block,
         ),
         name="near",
     )(shift, tree_vec, coords, order)
+    given = (leaf_skel, node_skel, sub_skel, jnp.asarray(skeleton_tables(rank)), leaf_maps, node_maps, bases)
+    items = (leaf_src.size + node_src.size + subtrees + 2) // 2 + AT_ONCE
+    sources = groups * leaves + 3 * groups + subtrees + 1
     return pl.pallas_call(
-        far_kernel,
+        functools.partial(far_kernel, groups, subtrees),
         out_shape=jax.ShapeDtypeStruct((nvec, rows_dev), F32),
-        in_specs=[smem] * 5 + [vmem] * 11,
+        in_specs=[smem] * 5 + [vmem] * 4 + [hbm] * 7,
         out_specs=vmem,
-        scratch_shapes=[
+        scratch_shapes=like(*given)
+        + [
             pltpu.VMEM((chunks * nvec, 2 * WIDE), BF16),
-            pltpu.VMEM((leaves, nvec, rank), F32),
-            pltpu.VMEM((subtrees, PACK_ROWS, 2 * rank), F32),
+            pltpu.VMEM((leaves + 2, nvec, rank), F32),
+            pltpu.VMEM((sources, PACK_ROWS, 2 * rank), F32),
+            pltpu.VMEM((leaves + 2, 2, rank, 2 * rank), F32),
+            pltpu.SMEM((2 * items,), jnp.int32),
+            pltpu.SMEM((items,), jnp.int32),
+            pltpu.SemaphoreType.DMA((7,)),
         ],
         compiler_params=params,
         name="far",
@@ -434,17 +507,11 @@
         leaf_count,
         node_src,
         node_count,
-        leaf_all.reshape(groups * leaves, PACK_ROWS, 2 * rank),
+        leaf_all,
         tree_all,
-        leaf_skel,
-        node_skel,
-        sub_skel,
         near,
         inverse,
-        bases,
-        leaf_maps,
-        node_maps,
-        jnp.asarray(skeleton_tables(rank)),
+        *given,
     )
 
 

time: 109 us -> 87.7 us (0.80)
  the two profiles are of different devices: /device:TPU:23 before, /device:TPU:0 now
where the time goes in v4:
time: 87.7 us; the launch traced here: 88.1 us
  Pallas kernels  56.7 us (65%)
  local copies, waits for them, and re-layouts  16.6 us (19%)
  starting transfers between devices  7.3 us (8%)
  blocking collectives  6.72 us (8%)
    pallas_call x1, Pallas kernels, shards(): pl.pallas_call(functools.partial(far_kernel, groups, subtrees), out_shape...  24.6 us
    pallas_call x1, Pallas kernels, shards(): pl.pallas_call(near_kernel, out_shape=(jax.ShapeDtypeStruct((leaves, nvec...  21.4 us
    unnamed x52, local copies, waits for them, and re-layouts  16.6 us
    pallas_call x1, Pallas kernels, shards(): pl.pallas_call(up_kernel, out_shape=(jax.ShapeDtypeStruct((leaves, nvec,...  10.7 us
    all_to_all x1, starting transfers between devices, shards(): tree_all = lax.all_to_all(tree_pack, ('leaf', 'grp'), 0, 0, tiled=True)  7.3 us
    all_gather x1, blocking collectives, shards(): leaf_all = lax.all_gather(leaf_pack, 'grp', axis=0, tiled=True)  6.72 us
  transfers between devices with their start and end apart: 1, of which 0 were waited for; matrix products, arithmetic and copies ran while one was open for 0% of the time, Pallas kernels for 24%

profile of v4, /device:TPU:0, one launch (start us, length us, event | category | flops | bytes accessed | tf_op | source)
XLA Modules:
  0.0 88.1 jit_solution(5188655878952999985)
XLA Ops:
  0.0 1.6 %copy-done = f32[16,64,512]{2,1,0:T(8,128)S(1)} copy-done((f32[16,64,512]{2,1,0:T(8,128)S(1)}, f32[16,64,512]{2,1,0:T(8,128)}, u32[]{:S(2)}) %copy-start) | copy-done | bytes 2097176
  1.6 1.0 %copy-done.2 = f32[16,64,64]{2,1,0:T(8,128)S(1)} copy-done((f32[16,64,64]{2,1,0:T(8,128)S(1)}, f32[16,64,64]{2,1,0:T(8,128)}, u32[]{:S(2)}) %copy-start.2) | copy-done | bytes 262168
  2.6 1.0 %copy-done.4 = f32[16,8192]{1,0:T(8,128)S(1)} copy-done((f32[16,8192]{1,0:T(8,128)S(1)}, f32[16,8192]{1,0:T(8,128)}, u32[]{:S(2)}) %copy-start.4) | copy-done | bytes 524312
  3.7 0.8 copy-done.8
  4.4 0.7 copy-done.10
  5.2 0.8 copy-done.12
  5.9 0.7 copy-done.17
  6.6 0.7 copy-done.19
  7.3 10.7 %up.1 = (f32[16,16,512]{2,1,0:T(8,128)S(1)}, f32[8,24,128]{2,1,0:T(8,128)S(1)}, f32[32,24,128]{2,1,0:T(8,128)}) custom-call(f32[16,8192]{1,0:T(8,128)S(1)} %copy-done.4, s32[64,128]{1,0:T(8,128)S(1)} %bitcast.3, f32[16,64,512]{2,1,0:T(8,128)S(1)} %copy-done, f32[16,64,64]{2,1,0:T(8,128)S(1)} %copy-done.2, f32[1,64,64]{2,1,0:T(8,128)S(1)} %copy-done.8, ...), custom_call_target="tpu_custom_call" | custom-call | tf_op jit(solution)/shard_map/up/pallas_call | solution.py:442
  18.0 0.0 copy-start.23
  18.0 0.8 copy-done.23
  18.8 7.3 %all-to-all-start = ((f32[32,24,128]{2,1,0:T(8,128)}), f32[32,24,128]{2,1,0:T(8,128)S(1)}, u32[]{:S(2)}, u32[]{:S(2)}) async-start(f32[32,24,128]{2,1,0:T(8,128)} %get-tuple-element.11), calls=%async_computation | async-start | bytes 786432 | tf_op jit(solution)/shard_map/all_to_all | solution.py:456
  26.8 0.0 copy-done.13
  26.8 0.0 copy-done.25
  26.8 0.0 copy-start.24
  26.8 1.0 %copy-done.24 = f32[16,16,512]{2,1,0:T(8,128)S(1)} copy-done((f32[16,16,512]{2,1,0:T(8,128)S(1)}, f32[16,16,512]{2,1,0:T(8,128)}, u32[]{:S(2)}) %copy-start.24) | copy-done | bytes 524312
  27.9 21.4 %near.1 = (f32[16,16,512]{2,1,0:T(8,128)S(1)}, s32[32,256]{1,0:T(8,128)S(1)}) custom-call(s32[1]{0:T(128)} %bitcast.2.shift, f32[16,16,512]{2,1,0:T(8,128)S(1)} %copy-done.24, f32[2,8192]{1,0:T(2,128)S(1)} %copy-done.25, s32[64,128]{1,0:T(8,128)S(1)} %bitcast.4), custom_call_target="tpu_custom_call" | custom-call | flops 536870912 | bytes 1048576 | tf_op jit(solution)/shard_map/near/pallas_call | solution.py:459
  49.3 0.0 copy-start.5
  49.3 0.8 copy-done.5
  50.1 0.6 copy-done.14
  50.7 6.7 %all_gather.3.refs_5_ = f32[32,24,128]{2,1,0:T(8,128)S(1)} all-gather(f32[8,24,128]{2,1,0:T(8,128)S(1)} %get-tuple-element.10), channel_id=1, replica_groups=mesh['leaf'=8,'grp'=4] {'grp'}, dimensions={0}, use_global_device_ids=true | all-gather | bytes 491520 | tf_op jit(solution)/shard_map/all_gather | solution.py:457
  57.4 0.0 all-to-all-done.refs_6_
  57.4 0.0 copy-start.6
  57.4 1.0 %copy-done.6 = f32[16,16,512]{2,1,0:T(8,128)S(1)} copy-done((f32[16,16,512]{2,1,0:T(8,128)S(1)}, f32[16,16,512]{2,1,0:T(8,128)}, u32[]{:S(2)}) %copy-start.6) | copy-done | bytes 524312
  58.5 0.9 %copy-done.7 = f32[6,64,128]{2,1,0:T(8,128)S(1)} copy-done((f32[6,64,128]{2,1,0:T(8,128)S(1)}, f32[6,64,128]{2,1,0:T(8,128)}, u32[]{:S(2)}) %copy-start.7) | copy-done | bytes 196632
  59.4 0.8 copy-done.15
  60.2 0.7 copy-done.16
  60.9 0.7 copy-done.18
  61.5 0.7 copy-done.20
  62.2 0.7 copy-done.21
  62.9 0.7 copy-done.22
  63.5 24.6 %far.1 = f32[16,8192]{1,0:T(8,128)} custom-call(s32[1]{0:T(128)} %bitcast.refs_0_, s32[16,16]{1,0:T(8,128)S(1)} %copy-done.16, s32[16]{0:T(128)S(1)} %copy-done.21, s32[1,8]{1,0:T(1,128)S(1)} %copy-done.22, s32[1]{0:T(128)S(6)} %copy.15.refs_4_, f32[32,24,128]{2,1,0:T(8,128)S(1)} %all_gather.3.refs_5_, f32[32,24,128]{2,1,0:T(8,128)S(1)} %all-to-all-done.refs_6_, ...), custom_call_target="tpu_custom_call" | custom-call | tf_op jit(solution)/shard_map/far/pallas_call | solution.py:487
  (26 shorter events, 0.0 us)
Async XLA Ops:
  0.0 1.6 %copy-start = (f32[16,64,512]{2,1,0:T(8,128)S(1)}, f32[16,64,512]{2,1,0:T(8,128)}, u32[]{:S(2)}) copy-start(f32[16,64,512]{2,1,0:T(8,128)} %refs_15_.1) | copy-start | bytes 6291460
  1.6 1.0 %copy-start.2 = (f32[16,64,64]{2,1,0:T(8,128)S(1)}, f32[16,64,64]{2,1,0:T(8,128)}, u32[]{:S(2)}) copy-start(f32[16,64,64]{2,1,0:T(8,128)} %refs_13_.1) | copy-start | bytes 786436
  2.6 1.0 %copy-start.4 = (f32[16,8192]{1,0:T(8,128)S(1)}, f32[16,8192]{1,0:T(8,128)}, u32[]{:S(2)}) copy-start(f32[16,8192]{1,0:T(8,128)} %refs_0_.1) | copy-start | bytes 1572868
  3.7 0.8 copy-start.8
  4.4 0.7 copy-start.10
  5.2 0.8 copy-start.12
  5.9 0.7 copy-start.17
  6.6 0.7 copy-start.19
  7.3 19.5 %copy-start.13 = (s32[8192]{0:T(1024)S(1)}, s32[8192]{0:T(1024)}, u32[]{:S(2)}) copy-start(s32[8192]{0:T(1024)} %param.16) | copy-start | bytes 98308
  7.3 19.5 %copy-start.25 = (f32[2,8192]{1,0:T(2,128)S(1)}, f32[2,8192]{1,0:T(2,128)}, u32[]{:S(2)}) copy-start(f32[2,8192]{1,0:T(2,128)} %crd_in.1) | copy-start | bytes 196612
  18.0 0.8 copy-start.23
  18.8 38.6 %all-to-all-start = ((f32[32,24,128]{2,1,0:T(8,128)}), f32[32,24,128]{2,1,0:T(8,128)S(1)}, u32[]{:S(2)}, u32[]{:S(2)}) async-start(f32[32,24,128]{2,1,0:T(8,128)} %get-tuple-element.11), calls=%async_computation | async-start | bytes 786432 | tf_op jit(solution)/shard_map/all_to_all | solution.py:456
  26.8 1.0 %copy-start.24 = (f32[16,16,512]{2,1,0:T(8,128)S(1)}, f32[16,16,512]{2,1,0:T(8,128)}, u32[]{:S(2)}) copy-start(f32[16,16,512]{2,1,0:T(8,128)} %copy-done.23) | copy-start | bytes 1572868
  27.8 29.6 %copy-start.1 = (f32[16,64,512]{2,1,0:T(8,128)S(1)}, f32[16,64,512]{2,1,0:T(8,128)}, u32[]{:S(2)}) copy-start(f32[16,64,512]{2,1,0:T(8,128)} %refs_15_.1) | copy-start | bytes 6291460
  27.8 29.6 %copy-start.3 = (f32[16,64,64]{2,1,0:T(8,128)S(1)}, f32[16,64,64]{2,1,0:T(8,128)}, u32[]{:S(2)}) copy-start(f32[16,64,64]{2,1,0:T(8,128)} %refs_13_.1) | copy-start | bytes 786436
  27.8 29.6 %copy-start.9 = (f32[1,64,64]{2,1,0:T(8,128)S(1)}, f32[1,64,64]{2,1,0:T(8,128)}, u32[]{:S(2)}) copy-start(f32[1,64,64]{2,1,0:T(8,128)} %refs_14_.1) | copy-start | bytes 49156
  27.8 29.6 %copy-start.11 = (f32[16,2,64]{2,1,0:T(2,128)S(1)}, f32[16,2,64]{2,1,0:T(2,128)}, u32[]{:S(2)}) copy-start(f32[16,2,64]{2,1,0:T(2,128)} %refs_9_.1) | copy-start | bytes 24580
  49.3 0.8 copy-start.5
  50.1 0.6 copy-start.14
  57.4 1.0 %copy-start.6 = (f32[16,16,512]{2,1,0:T(8,128)S(1)}, f32[16,16,512]{2,1,0:T(8,128)}, u32[]{:S(2)}) copy-start(f32[16,16,512]{2,1,0:T(8,128)} %copy-done.5) | copy-start | bytes 1572868
  58.5 0.9 %copy-start.7 = (f32[6,64,128]{2,1,0:T(8,128)S(1)}, f32[6,64,128]{2,1,0:T(8,128)}, u32[]{:S(2)}) copy-start(f32[6,64,128]{2,1,0:T(8,128)} %constant.25.clone.refs_12_) | copy-start | bytes 589828
  59.4 0.8 copy-start.15
  60.2 0.7 copy-start.16
  60.9 0.7 copy-start.18
  61.5 0.7 copy-start.20
  62.2 0.7 copy-start.21
  62.9 0.7 copy-start.22
